TPU v7x, 256 devices: a whole 4x4x8 slice. The times are simulated.
256 devices in a mesh: face: 8 (over x, y_hi), tile: 32 (over y_lo, z, core).
Axes of the slice: x: 4, y: 4 (y_hi: 2, y_lo: 2; y = y_hi * 2 + y_lo), z: 8, core: 2. Of those that a mesh axis runs over, the one named last changes fastest.
Arguments:
- features: bfloat16 [8, 256, 256, 256], P('face', 'tile'), may hold values from -2000 to 2000
- cotangent: bfloat16 [8, 256, 256, 256], P('face', 'tile'), may hold values from -10 to 10
- w_fine: bfloat16 [9, 256, 256], replicated, may hold values from -0.125 to 0.125
- w_coarse: bfloat16 [9, 256, 256], replicated, may hold values from -0.125 to 0.125
- gain: float32 [256], replicated, may hold values from 0.1 to 1.9
- neighbors: int32 [8, 4], replicated, may hold values from 0 to 7, as said below
- neighbor_edges: int32 [8, 4], replicated, may hold values from 0 to 3, as said below
Outputs:
- output: bfloat16 [8, 256, 256, 256], P('face', 'tile')
- grad_features: float32 [8, 256, 256, 256], P('face', 'tile')
- grad_w_fine: float32 [9, 256, 256], P(None, 'tile')
- grad_w_coarse: float32 [9, 256, 256], P(None, 'tile')
- grad_gain: float32 [256], replicated
Inputs may be any that keep to these rules, and one draw needn't show every extreme that they name: The right edge of face f meets the left edge of face neighbors[f,1], and the left neighbours name f back; these column gluings form one cycle through all faces. Top and bottom edges are glued in pairs: the face named at an edge names f back at the edge given by neighbor_edges. A face's top may meet its own bottom. neighbor_edges[f,1] is 3 and neighbor_edges[f,3] is 1; the entries at the top and bottom edges are 0 or 2.
All inputs are finite; a program needn't handle non-finite values.
Results may differ from a plain program's by a relative error of at most 0.012.
Values may be sent and summed in bfloat16 or wider, within the bound.
A program may use at most 128 MiB of HBM per device.

v0:
```python
import jax
import jax.numpy as jnp
from jax import lax
from jax.sharding import PartitionSpec as P

GROUPS = 32


def with_halo(array, sides, width):
    for axis, dim in sides:
        count, length = (lax.axis_size(axis), array.shape[dim])
        up = [(i, (i + 1) % count) for i in range(count)]
        down = [(j, i) for i, j in up]
        last = lax.slice_in_dim(array, length - width, length, axis=dim)
        initial = lax.slice_in_dim(array, 0, width, axis=dim)
        before = lax.ppermute(last, axis, up)
        after = lax.ppermute(initial, axis, down)
        array = jnp.concatenate([before, array, after], axis=dim)
    return array


def silu_slope(values):
    sigma = jax.nn.sigmoid(values)
    return sigma * (1.0 + values * (1.0 - sigma))


def row_halo(field):
    return with_halo(field, (("tile", 0),), 1)


def rim_flags():
    tile_index = lax.axis_index("tile")
    return (tile_index == 0, tile_index == lax.axis_size("tile") - 1)


def glue(sides, rims, neighbors, neighbor_edges):
    face_index = lax.axis_index("face")
    left_face = neighbors[face_index, 3]
    right_face = neighbors[face_index, 1]
    top_face = neighbors[face_index, 0]
    bottom_face = neighbors[face_index, 2]
    top_edge = neighbor_edges[face_index, 0]
    bottom_edge = neighbor_edges[face_index, 2]
    all_sides, all_rims = (
        lax.all_gather(sides[None], "face", axis=0, tiled=True),
        lax.all_gather(rims[None], "face", axis=0, tiled=True),
    )
    top_source = all_rims[top_face]
    bottom_source = all_rims[bottom_face]
    top_plain = jnp.where(top_edge == 2, top_source[1], top_source[0])
    bottom_plain = jnp.where(bottom_edge == 0, bottom_source[0], bottom_source[1])
    left_side = all_sides[left_face, 1]
    right_side = all_sides[right_face, 0]
    top_side = jnp.where(top_edge == 2, top_plain, top_plain[::-1])
    bottom_side = jnp.where(bottom_edge == 0, bottom_plain, bottom_plain[::-1])
    return (left_side, right_side, top_side, bottom_side)


def glued_pad(field, neighbors, neighbor_edges):
    n_rows = field.shape[0]
    extended = row_halo(field)
    is_first, is_final = rim_flags()
    top_row = jnp.where(is_first, extended[1], extended[n_rows + 1])
    bottom_row = jnp.where(is_first, extended[0], extended[n_rows])
    sides = jnp.stack([extended[:, 0], extended[:, -1]])
    rims = jnp.stack([top_row, bottom_row])
    left_side, right_side, top_side, bottom_side = glue(sides, rims, neighbors, neighbor_edges)
    upper = jnp.where(is_first, top_side, extended[0])
    lower = jnp.where(is_final, bottom_side, extended[n_rows + 1])
    inner = jnp.concatenate([upper[None], extended[1 : n_rows + 1], lower[None]], axis=0)
    position = jnp.arange(n_rows + 2)
    corner = (position == 0) & is_first | (position == n_rows + 1) & is_final
    left_side = jnp.where(corner[:, None], jnp.zeros_like(left_side), left_side)
    right_side = jnp.where(corner[:, None], jnp.zeros_like(right_side), right_side)
    return jnp.concatenate([left_side[:, None], inner, right_side[:, None]], axis=1)


def convolve(padded, weights):
    n_rows = padded.shape[0] - 2
    n_cols = padded.shape[1] - 2
    total = jnp.zeros((n_rows, n_cols, weights.shape[2]), jnp.float32)
    for tap in range(9):
        row_step, col_step = divmod(tap, 3)
        tap_slice = padded[row_step : row_step + n_rows, col_step : col_step + n_cols]
        total = total + jnp.dot(tap_slice, weights[tap], preferred_element_type=jnp.float32)
    return total


def convolve_back(grad, weights, neighbors, neighbor_edges):
    n_rows, n_cols, chans = grad.shape
    extended = row_halo(grad)
    is_first, is_final = rim_flags()
    top_source = jnp.where(is_first, extended[1], extended[n_rows + 1])
    bottom_source = jnp.where(is_first, extended[0], extended[n_rows])
    upper = jnp.where(is_first, jnp.zeros_like(extended[0]), extended[0])
    lower = jnp.where(is_final, jnp.zeros_like(extended[0]), extended[n_rows + 1])
    inner = jnp.concatenate([upper[None], extended[1 : n_rows + 1], lower[None]], axis=0)
    widened = jnp.pad(inner, ((0, 0), (2, 2), (0, 0)))
    full = jnp.zeros((n_rows, n_cols + 2, weights.shape[1]), jnp.float32)
    for tap in range(9):
        row_step = tap // 3 - 1
        col_step = tap % 3 - 1
        tap_slice = widened[
            1 - row_step : 1 - row_step + n_rows, 1 - col_step : 1 - col_step + n_cols + 2
        ]
        full = full + jnp.dot(tap_slice, weights[tap].T, preferred_element_type=jnp.float32)
    top_wide = jnp.pad(top_source, ((1, 1), (0, 0)))
    bottom_wide = jnp.pad(bottom_source, ((1, 1), (0, 0)))
    top_grad = jnp.zeros((n_cols, weights.shape[1]), jnp.float32)
    bottom_grad = jnp.zeros((n_cols, weights.shape[1]), jnp.float32)
    for col_step in (-1, 0, 1):
        top_grad = top_grad + jnp.dot(
            top_wide[1 - col_step : 1 - col_step + n_cols],
            weights[col_step + 1].T,
            preferred_element_type=jnp.float32,
        )
        bottom_grad = bottom_grad + jnp.dot(
            bottom_wide[1 - col_step : 1 - col_step + n_cols],
            weights[col_step + 7].T,
            preferred_element_type=jnp.float32,
        )
    sides = jnp.pad(
        jnp.stack([full[:, 0], full[:, -1]]).astype(jnp.bfloat16), ((0, 0), (1, 1), (0, 0))
    )
    rims = jnp.stack([top_grad, bottom_grad]).astype(jnp.bfloat16)
    left_side, right_side, top_side, bottom_side = glue(sides, rims, neighbors, neighbor_edges)
    result = full[:, 1:-1]
    result = result.at[:, 0].add(left_side[1 : n_rows + 1].astype(jnp.float32))
    result = result.at[:, -1].add(right_side[1 : n_rows + 1].astype(jnp.float32))
    result = result.at[0].add(jnp.where(is_first, top_side.astype(jnp.float32), 0.0))
    result = result.at[-1].add(jnp.where(is_final, bottom_side.astype(jnp.float32), 0.0))
    return result


def weight_terms(padded, grad):
    n_rows, n_cols = (grad.shape[0], grad.shape[1])
    terms = []
    for tap in range(9):
        row_step, col_step = divmod(tap, 3)
        tap_slice = padded[row_step : row_step + n_rows, col_step : col_step + n_cols]
        terms.append(
            lax.dot_general(
                tap_slice, grad, (((0, 1), (0, 1)), ((), ())), preferred_element_type=jnp.float32
            )
        )
    return jnp.stack(terms)


def reduce_weights(local_terms):
    share_rows = local_terms.shape[1] // lax.axis_size("tile")
    summed = lax.psum(local_terms, ("face", "tile"))
    return lax.dynamic_slice_in_dim(summed, lax.axis_index("tile") * share_rows, share_rows, 1)


def pool_sum(values):
    n_rows, n_cols, chans = values.shape
    return jnp.sum(values.reshape(n_rows // 2, 2, n_cols // 2, 2, chans), axis=(1, 3))


def upsample(values):
    return jnp.repeat(jnp.repeat(values, 2, axis=0), 2, axis=1)


def on_device(features, cotangent, w_fine, w_coarse, gain, neighbors, neighbor_edges):
    field = features[0]
    n_rows, n_cols, chans = field.shape
    group_size = chans // GROUPS
    cells = lax.axis_size("face") * n_cols * n_cols
    count = cells * group_size
    values = field.astype(jnp.float32)
    chan_sums, chan_squares = lax.psum(
        (jnp.sum(values, axis=(0, 1)), jnp.sum(values * values, axis=(0, 1))), ("face", "tile")
    )
    group_mean = jnp.sum(chan_sums.reshape(GROUPS, group_size), axis=1) / count
    second = jnp.sum(chan_squares.reshape(GROUPS, group_size), axis=1) / count
    inverse = lax.rsqrt(second - group_mean * group_mean + 1e-05)
    mean_chan = jnp.repeat(group_mean, group_size)
    inverse_chan = jnp.repeat(inverse, group_size)
    normed = (values - mean_chan) * inverse_chan
    act = normed * gain
    hidden = jax.nn.silu(act).astype(jnp.bfloat16)
    hidden_pad = glued_pad(hidden, neighbors, neighbor_edges)
    fine = convolve(hidden_pad, w_fine).astype(jnp.bfloat16)
    pooled = pool_sum(fine.astype(jnp.float32)) * 0.25
    coarse_in = jax.nn.silu(pooled).astype(jnp.bfloat16)
    coarse_pad = glued_pad(coarse_in, neighbors, neighbor_edges)
    coarse_out = convolve(coarse_pad, w_coarse)
    output = (fine.astype(jnp.float32) + upsample(coarse_out)).astype(jnp.bfloat16)
    upstream = cotangent[0].astype(jnp.float32)
    grad_coarse_out = pool_sum(upstream).astype(jnp.bfloat16)
    coarse_terms = weight_terms(coarse_pad, grad_coarse_out)
    grad_coarse_in = convolve_back(grad_coarse_out, w_coarse, neighbors, neighbor_edges)
    grad_pooled = grad_coarse_in * silu_slope(pooled)
    grad_fine = (upstream + upsample(grad_pooled) * 0.25).astype(jnp.bfloat16)
    grad_w_coarse = reduce_weights(coarse_terms) / cells
    fine_terms = weight_terms(hidden_pad, grad_fine)
    grad_hidden = convolve_back(grad_fine, w_fine, neighbors, neighbor_edges)
    grad_act = grad_hidden * silu_slope(act)
    slope_sum, shift_sum = lax.psum(
        (jnp.sum(grad_act * normed, axis=(0, 1)), jnp.sum(grad_act, axis=(0, 1))), ("face", "tile")
    )
    grad_w_fine = reduce_weights(fine_terms) / cells
    grad_gain = slope_sum / cells
    group_shift = jnp.sum((gain * shift_sum).reshape(GROUPS, group_size), axis=1) / count
    group_slope = jnp.sum((gain * slope_sum).reshape(GROUPS, group_size), axis=1) / count
    grad_features = inverse_chan * (
        gain * grad_act
        - jnp.repeat(group_shift, group_size)
        - normed * jnp.repeat(group_slope, group_size)
    )
    return (output[None], grad_features[None], grad_w_fine, grad_w_coarse, grad_gain)


def solution(mesh):
    return jax.shard_map(
        on_device,
        mesh=mesh,
        in_specs=(
            P("face", "tile", None, None),
            P("face", "tile", None, None),
            P(),
            P(),
            P(),
            P(),
            P(),
        ),
        out_specs=(
            P("face", "tile", None, None),
            P("face", "tile", None, None),
            P(None, "tile", None),
            P(None, "tile", None),
            P(),
        ),
        check_vma=False,
    )
```

profile of v0, /device:TPU:4, one launch (start us, length us, event | category | flops | bytes accessed | tf_op | source)
XLA Modules:
  0.0 702.7 jit_solution(8862378347655588694)
XLA Ops:
  7.2 1.5 squeeze.92
  8.8 1.8 reduce_sum.98
  11.3 6.3 collective-permute-start.5
  18.4 73.5 %all-reduce.9 = (f32[32,8]{1,0:T(8,128)S(1)}, f32[32,8]{1,0:T(8,128)S(1)}) all-reduce(f32[32,8]{1,0:T(8,128)S(1)} %reshape.594, f32[32,8]{1,0:T(8,128)S(1)} %reshape.593), channel_id=1, replica_groups=mesh['face'=8,'tile'=32] {'face','tile'}, use_global_device_ids=true, to_apply=%region_4.0 | all-reduce | flops 512 | bytes 4096 | tf_op jit(solution)/shard_map/psum | solution.py:171
  100.1 3.1 fusion.193
  107.0 0.9 select_bitcast_fusion.3
  108.5 5.2 collective-permute-done.4
  116.9 5.3 collective-permute-done
  125.1 32.1 %all-gather.4 = bf16[16,6,256]{2,1,0:T(8,128)(2,1)S(1)} all-gather(bf16[2,6,256]{2,1,0:T(8,128)(2,1)S(1)} %fusion.286), channel_id=6, replica_groups=mesh['face'=8,'tile'=32] {'face'}, dimensions={0}, use_global_device_ids=true | all-gather | bytes 55296 | tf_op jit(solution)/shard_map/all_gather | solution.py:45
  158.1 34.9 %all-gather = bf16[16,10,256]{2,1,0:T(8,128)(2,1)S(1)} all-gather(bf16[2,10,256]{2,1,0:T(8,128)(2,1)S(1)} %pad_maximum_fusion.18), channel_id=2, replica_groups=mesh['face'=8,'tile'=32] {'face'}, dimensions={0}, use_global_device_ids=true | all-gather | bytes 92160 | tf_op jit(solution)/shard_map/all_gather | solution.py:45
  193.2 1.0 fusion.265
  194.5 30.5 %all-gather.15.cloned.1.call-done = bf16[16,256,256]{2,1,0:T(8,128)(2,1)} async-done(((bf16[2,256,256]{2,1,0:T(8,128)(2,1)}), bf16[16,256,256]{2,1,0:T(8,128)(2,1)}) %all-gather.15.cloned.1.call-update) | async-done | bytes 2097168 | tf_op jit(solution)/shard_map/all_gather | solution.py:46
  225.0 1.1 fusion.152
  226.5 1.0 fusion.207
  231.9 1.1 copy-done.22
  233.1 2.4 fusion.36
  235.5 3.5 reshape.595
  238.9 3.9 reduce_sum.97
  242.8 1.3 multiply_multiply_fusion
  244.2 2.1 broadcast_in_dim.126
  246.3 3.7 mul.153
  250.0 3.7 mul.165
  253.7 1.7 collective-permute-start.3
  255.4 2.1 fusion.4
  261.1 1.1 fusion.59
  264.3 1.4 copy-done.21
  265.8 1.0 fusion.166
  266.9 3.9 collective-permute-start.7
  272.4 32.1 %all-gather.2 = bf16[16,6,256]{2,1,0:T(8,128)(2,1)S(1)} all-gather(bf16[2,6,256]{2,1,0:T(8,128)(2,1)S(1)} %pad_maximum_fusion.22), channel_id=4, replica_groups=mesh['face'=8,'tile'=32] {'face'}, dimensions={0}, use_global_device_ids=true | all-gather | bytes 55296 | tf_op jit(solution)/shard_map/all_gather | solution.py:45
  304.6 1.1 fusion.202
  305.8 1.1 convolution_add_fusion.13
  307.9 5.7 collective-permute-done.6
  317.9 1.1 fusion.316
  319.3 1.1 copy-done.9
  320.4 34.1 %all-gather.5 = bf16[16,10,256]{2,1,0:T(8,128)(2,1)S(1)} all-gather(bf16[2,10,256]{2,1,0:T(8,128)(2,1)S(1)} %fusion.282), channel_id=7, replica_groups=mesh['face'=8,'tile'=32] {'face'}, dimensions={0}, use_global_device_ids=true | all-gather | bytes 92160 | tf_op jit(solution)/shard_map/all_gather | solution.py:45
  356.6 0.9 slice_add_fusion.5
  358.6 1.9 fusion.268
  360.5 1.4 rev.26
  361.9 1.4 rev.27
  363.3 0.9 fusion.270
  364.2 0.9 fusion.269
  365.2 0.8 maximum_maximum_fusion.1
  368.9 2.5 reshape.597
  371.3 1.0 fusion.53
  372.3 1.0 fusion.46
  373.3 1.0 fusion.52
  374.3 1.0 fusion.51
  375.3 1.0 fusion.50
  376.3 1.0 fusion.49
  377.3 1.0 fusion.48
  378.2 1.0 fusion.45
  379.2 1.0 fusion.47
  380.2 1.6 copy-done.3
  381.8 2.8 fusion.88
  384.6 30.9 %all-gather.13.cloned.1.call-done = bf16[8,2,256,256]{3,2,1,0:T(8,128)(2,1)} async-done(((bf16[1,2,256,256]{3,2,1,0:T(8,128)(2,1)}), bf16[8,2,256,256]{3,2,1,0:T(8,128)(2,1)}) %all-gather.13.cloned.1.call-update) | async-done | bytes 2097168 | tf_op jit(solution)/shard_map/all_gather | solution.py:46
  415.5 1.1 fusion.147
  417.0 1.7 fusion.128
  418.7 1.7 fusion.127
  420.4 2.7 fusion.311
  423.1 75.8 %all-reduce.8 = (f32[256]{0:T(256)S(1)}, f32[256]{0:T(256)S(1)}) all-reduce(f32[256]{0:T(256)S(1)} %get-tuple-element.102, f32[256]{0:T(256)S(1)} %get-tuple-element.101), channel_id=1, replica_groups=mesh['face'=8,'tile'=32] {'face','tile'}, use_global_device_ids=true, to_apply=%region_12.13 | all-reduce | flops 512 | bytes 4096 | tf_op jit(solution)/shard_map/psum | solution.py:199
  500.3 1.9 fusion.23
  502.2 190.8 %all-reduce.13.cloned.1.call-done = (f32[9,256,256]{2,1,0:T(8,128)}, f32[9,256,256]{2,1,0:T(8,128)}) async-done(((f32[9,256,256]{2,1,0:T(8,128)}, f32[9,256,256]{2,1,0:T(8,128)}), (f32[9,256,256]{2,1,0:T(8,128)}, f32[9,256,256]{2,1,0:T(8,128)})) %all-reduce.13.cloned.1.call-update) | async-done | bytes 4718608 | tf_op jit(solution)/shard_map/psum | solution.py:151
  692.9 1.5 dynamic-slice_multiply_fusion
  694.4 1.5 dynamic-slice_multiply_fusion.1
  (245 shorter events, 37.7 us)
Async XLA Ops:
  7.2 10.5 %copy-start = (bf16[1,8,256,256]{3,2,1,0:T(8,128)(2,1)S(1)}, bf16[1,8,256,256]{3,2,1,0:T(8,128)(2,1)}, u32[]{:S(2)}) copy-start(bf16[1,8,256,256]{3,2,1,0:T(8,128)(2,1)} %param.23) | copy-start | bytes 3145732
  7.2 186.0 %all-gather.11.cloned.1.call-start = ((), (), s32[]{:S(2)}) async-start(), calls=%async_computation | async-start | bytes 1179648 | tf_op jit(solution)/shard_map/all_gather | solution.py:46
  8.8 83.8 %copy-start.41 = (f32[256]{0:T(256)S(1)}, f32[256]{0:T(256)}, u32[]{:S(2)}) copy-start(f32[256]{0:T(256)} %param.27) | copy-start | bytes 3076
  10.6 105.1 %copy-start.14 = (bf16[4,128,256]{2,1,0:T(8,128)(2,1)}, bf16[4,128,256]{2,1,0:T(8,128)(2,1)S(1)}, u32[]{:S(2)}) copy-start(bf16[4,128,256]{2,1,0:T(8,128)(2,1)S(1)} %reduce_sum.98) | copy-start | bytes 786436
  11.3 83.1 %copy-start.43 = (s32[8,4]{0,1:T(4,128)S(1)}, s32[8,4]{0,1:T(4,128)}, u32[]{:S(2)}) copy-start(s32[8,4]{0,1:T(4,128)} %param.28) | copy-start | bytes 388
  11.3 83.1 %copy-start.44 = (s32[8,4]{0,1:T(4,128)S(1)}, s32[8,4]{0,1:T(4,128)}, u32[]{:S(2)}) copy-start(s32[8,4]{0,1:T(4,128)} %param.29) | copy-start | bytes 388
  11.3 95.6 %collective-permute-start.5 = (bf16[1,128,256]{2,1,0:T(8,128)(2,1)}, bf16[1,128,256]{2,1,0:T(8,128)(2,1)}, u32[]{:S(2)}, u32[]{:S(2)}) collective-permute-start(bf16[1,128,256]{2,1,0:T(8,128)(2,1)} %slice.693), channel_id=1, source_target_pairs={{1,0},{2,1},{3,2},{4,3},{5,4},{6,5},{7,6},{8,7},{9,8},{10,9},{11,1... | collective-permute-start | bytes 196616 | tf_op jit(solution)/shard_map/ppermute | solution.py:17
  92.4 167.6 %copy-start.37 = (f32[256]{0:T(256)}, f32[256]{0:T(256)S(1)}, u32[]{:S(2)}) copy-start(f32[256]{0:T(256)S(1)} %mul.134) | copy-start | bytes 3076
  92.5 167.4 %copy-start.39 = (f32[256]{0:T(256)}, f32[256]{0:T(256)S(1)}, u32[]{:S(2)}) copy-start(f32[256]{0:T(256)S(1)} %sub.38) | copy-start | bytes 3076
  93.9 21.7 %collective-permute-start.1 = (bf16[1,256,256]{2,1,0:T(8,128)(2,1)}, bf16[1,256,256]{2,1,0:T(8,128)(2,1)}, u32[]{:S(2)}, u32[]{:S(2)}) collective-permute-start(bf16[1,256,256]{2,1,0:T(8,128)(2,1)} %slice.677), channel_id=1, source_target_pairs={{1,0},{2,1},{3,2},{4,3},{5,4},{6,5},{7,6},{8,7},{9,8},{10,9},{11,1... | collective-permute-start | bytes 393224 | tf_op jit(solution)/shard_map/ppermute | solution.py:17
  100.0 7.9 %copy-start.10 = (bf16[9,256,256]{2,1,0:T(8,128)(2,1)S(1)}, bf16[9,256,256]{2,1,0:T(8,128)(2,1)}, u32[]{:S(2)}) copy-start(bf16[9,256,256]{2,1,0:T(8,128)(2,1)} %param.26) | copy-start | bytes 3538948
  107.8 5.9 collective-permute-start.4
  115.0 110.0 %all-gather.15.cloned.1.call-start = ((), (), s32[]{:S(2)}) async-start(), calls=%async_computation.2 | async-start | bytes 2359296 | tf_op jit(solution)/shard_map/all_gather | solution.py:46
  115.6 6.6 collective-permute-start
  122.2 0.6 copy-start.25
  123.6 235.0 %all-gather.17.cloned.1.call-start = ((), (), s32[]{:S(2)}) async-start(), calls=%async_computation.3 | async-start | bytes 1179648 | tf_op jit(solution)/shard_map/all_gather | solution.py:46
  124.5 32.9 %copy-start.26 = (bf16[1,256,256]{2,1,0:T(8,128)(2,1)S(1)}, bf16[1,256,256]{2,1,0:T(8,128)(2,1)}, u32[]{:S(2)}) copy-start(bf16[1,256,256]{2,1,0:T(8,128)(2,1)} %copy-done.25) | copy-start | bytes 393220
  226.5 4.5 copy-start.29
  227.5 4.0 copy-start.27
  227.5 1.3 copy-start.12
  228.2 3.8 copy-start.6
  231.5 1.6 copy-start.22
  244.1 9.5 %copy-start.4 = (bf16[4,128,256]{2,1,0:T(8,128)(2,1)}, bf16[4,128,256]{2,1,0:T(8,128)(2,1)S(1)}, u32[]{:S(2)}) copy-start(bf16[4,128,256]{2,1,0:T(8,128)(2,1)S(1)} %get-tuple-element.129) | copy-start | bytes 786436
  253.7 12.0 %collective-permute-start.3 = (bf16[1,128,256]{2,1,0:T(8,128)(2,1)S(1)}, bf16[1,128,256]{2,1,0:T(8,128)(2,1)S(1)}, u32[]{:S(2)}, u32[]{:S(2)}) collective-permute-start(bf16[1,128,256]{2,1,0:T(8,128)(2,1)S(1)} %slice.685), channel_id=1, source_target_pairs={{1,0},{2,1},{3,2},{4,3},{5,4},{6,5},{7,6},{8,7},{9,8},{10,9},{11,1... | collective-permute-start | bytes 196616 | tf_op jit(solution)/shard_map/ppermute | solution.py:17
  257.5 0.9 copy-start.30
  257.5 1.4 copy-start.7
  258.9 1.2 copy-start.1
  258.9 1.5 copy-start.16
  258.9 2.2 copy-start.23
  262.2 1.0 copy-start.28
  263.7 2.0 copy-start.5
  263.8 2.1 copy-start.11
  264.3 1.4 copy-start.21
  265.7 5.9 copy-start.33
  265.7 41.3 %copy-start.45 = (pred[6]{0:T(512)(128)(4,1)S(1)}, pred[6]{0:T(512)(128)(4,1)}, u32[]{:S(2)}) copy-start(pred[6]{0:T(512)(128)(4,1)} %and_or_fusion) | copy-start | bytes 22
  265.7 5.9 collective-permute-start.2
  266.9 37.7 %collective-permute-start.7 = (bf16[1,256,256]{2,1,0:T(8,128)(2,1)S(1)}, bf16[1,256,256]{2,1,0:T(8,128)(2,1)S(1)}, u32[]{:S(2)}, u32[]{:S(2)}) collective-permute-start(bf16[1,256,256]{2,1,0:T(8,128)(2,1)S(1)} %slice.711), channel_id=1, source_target_pairs={{1,0},{2,1},{3,2},{4,3},{5,4},{6,5},{7,6},{8,7},{9,8},{10,9},{11,1... | collective-permute-start | bytes 393224 | tf_op jit(solution)/shard_map/ppermute | solution.py:17
  271.6 33.0 %copy-start.34 = (bf16[1,128,256]{2,1,0:T(8,128)(2,1)}, bf16[1,128,256]{2,1,0:T(8,128)(2,1)S(1)}, u32[]{:S(2)}) copy-start(bf16[1,128,256]{2,1,0:T(8,128)(2,1)S(1)} %collective-permute-done.2) | copy-start | bytes 196612
  272.4 143.1 %all-gather.13.cloned.1.call-start = ((), (), s32[]{:S(2)}) async-start(), calls=%async_computation.1 | async-start | bytes 2359296 | tf_op jit(solution)/shard_map/all_gather | solution.py:46
  272.4 35.3 %copy-start.13 = (bf16[9,256,256]{2,1,0:T(8,128)(2,1)S(1)}, bf16[9,256,256]{2,1,0:T(8,128)(2,1)}, u32[]{:S(2)}) copy-start(bf16[9,256,256]{2,1,0:T(8,128)(2,1)} %param.25) | copy-start | bytes 3538948
  306.9 6.7 collective-permute-start.6
  319.0 1.4 copy-start.9
  357.4 335.5 %all-reduce.13.cloned.1.call-start = ((), (), s32[]{:S(2)}) async-start(), calls=%async_computation.4 | async-start | bytes 9437184 | tf_op jit(solution)/shard_map/psum | solution.py:151
  358.5 8.0 %copy-start.8 = (f32[8,256,256]{2,1,0:T(8,128)}, f32[8,256,256]{2,1,0:T(8,128)S(1)}, u32[]{:S(2)}) copy-start(f32[8,256,256]{2,1,0:T(8,128)S(1)} %scatter-add.35) | copy-start | bytes 6291460
  364.2 3.2 copy-start.31
  365.2 2.6 copy-start.35
  366.0 1.2 copy-start.17
  366.0 1.2 copy-start.19
  366.3 1.2 copy-start.24
  368.8 2.5 copy-start.15
  368.9 2.5 copy-start.20
  368.9 3.5 copy-start.32
  368.9 4.5 copy-start.18
  373.3 4.9 copy-start.36
  380.2 1.6 copy-start.3
  384.6 35.8 %copy-start.2 = (bf16[1,8,256,256]{3,2,1,0:T(8,128)(2,1)S(1)}, bf16[1,8,256,256]{3,2,1,0:T(8,128)(2,1)}, u32[]{:S(2)}) copy-start(bf16[1,8,256,256]{3,2,1,0:T(8,128)(2,1)} %param.23) | copy-start | bytes 3145732
  384.6 35.8 %copy-start.38 = (f32[256]{0:T(256)S(1)}, f32[256]{0:T(256)}, u32[]{:S(2)}) copy-start(f32[256]{0:T(256)} %copy-done.37) | copy-start | bytes 3076
  384.6 35.8 %copy-start.40 = (f32[256]{0:T(256)S(1)}, f32[256]{0:T(256)}, u32[]{:S(2)}) copy-start(f32[256]{0:T(256)} %copy-done.39) | copy-start | bytes 3076
  384.6 35.8 %copy-start.42 = (f32[256]{0:T(256)S(1)}, f32[256]{0:T(256)}, u32[]{:S(2)}) copy-start(f32[256]{0:T(256)} %param.27) | copy-start | bytes 3076
Sparse Core Ops, SparseCore 0:
  115.1 47.4 all-gather.10
  165.8 59.1 all-gather.14
  272.5 50.5 all-gather.16
  357.6 57.8 all-gather.12
  420.9 271.9 all-reduce.12
where the time goes:
time: 712 us; the launch traced here: 703 us
  blocking collectives  283 us (40%)
  waiting for transfers between devices  269 us (38%)
  other arithmetic  42.6 us (6%)
  matrix products  37 us (5%)
  local copies, waits for them, and re-layouts  34.3 us (5%)
  between operations  24 us (3%)
  starting transfers between devices  13 us (2%)
    psum x1, waiting for transfers between devices, reduce_weights(): summed = lax.psum(local_terms, ('face', 'tile'))  191 us
    all_gather x4, blocking collectives, glue(): lax.all_gather(sides[None], 'face', axis=0, tiled=True)  133 us
    psum x1, blocking collectives, on_device(): lax.psum((jnp.sum(grad_act * normed, axis=(0, 1)), jnp.sum(grad_act, axis...  75.8 us
    psum x1, blocking collectives, on_device(): lax.psum((jnp.sum(values, axis=(0, 1)), jnp.sum(values * values, axis=(0,...  73.5 us
    all_gather x4, waiting for transfers between devices, glue(): lax.all_gather(rims[None], 'face', axis=0, tiled=True)  61.4 us
    ppermute x4, waiting for transfers between devices, with_halo(): before = lax.ppermute(last, axis, up)  16.9 us
  transfers between devices with their start and end apart: 13, of which 7 were waited for; matrix products, arithmetic and copies ran while one was open for 10% of the time, Pallas kernels for 0%

commit v1 on v0

v1 whole, which is shorter than its diff:
```python
import functools

import jax
import jax.numpy as jnp
from jax import lax
from jax.experimental import pallas as pl
from jax.experimental.pallas import tpu as pltpu
from jax.sharding import PartitionSpec as P

BF = jnp.bfloat16
F32 = jnp.float32
MESH = pl.DeviceIdType.MESH
NF = 8
NT = 32
NZ = 16
RD = 8
FS = 256
CS = 128
C = 256
GROUP = 8
SLOTS = 16
CELLS = NF * FS * FS
VMEM_LIMIT = 60 * 1024 * 1024

VM = pl.BlockSpec(memory_space=pltpu.VMEM)
SM = pl.BlockSpec(memory_space=pltpu.SMEM)
DMA = pltpu.SemaphoreType.DMA


def remote(src, dst, send, recv, face, tile):
    return pltpu.make_async_remote_copy(
        src_ref=src,
        dst_ref=dst,
        send_sem=send,
        recv_sem=recv,
        device_id=(face, tile),
        device_id_type=MESH,
    )


def place():
    return lax.axis_index("face"), lax.axis_index("tile")


def is_rim(tile):
    return (tile == 0) | (tile == NT - 1)


def slot_device(slot):
    return lax.div(slot, 2), (NT - 1) * lax.rem(slot, 2)


def my_slot(face, tile):
    return 2 * face + jnp.where(tile == NT - 1, 1, 0)


def multiple(value, of):
    return pl.multiple_of(value * of, of)


def signal(barrier, face, tile):
    pl.semaphore_signal(barrier, inc=1, device_id=(face, tile), device_id_type=MESH)


def line_a(face, tile, step):
    mine = lax.rem(tile, NZ)
    other = lax.rem(mine + step, NZ)
    return mine, other, (face, tile - mine + other)


def line_b(face, tile, step):
    mine = face * 2 + lax.div(tile, NZ)
    other = lax.rem(mine + step, 2 * NF)
    return mine, other, (lax.div(other, 2), lax.rem(other, 2) * NZ + lax.rem(tile, NZ))


def barrier_signal(halos):
    face, tile = place()
    barrier = pltpu.get_barrier_semaphore()

    @pl.loop(1, NZ)
    def _(step):
        for line in (line_a, line_b):
            _, _, device = line(face, tile, step)
            signal(barrier, *device)

    if halos:
        signal(barrier, face, lax.rem(tile + 1, NT))
        signal(barrier, face, lax.rem(tile + NT - 1, NT))

        @pl.when(is_rim(tile))
        def _():
            mine = my_slot(face, tile)

            @pl.loop(1, SLOTS)
            def _(step):
                signal(barrier, *slot_device(lax.rem(mine + step, SLOTS)))


def barrier_wait(halos, more=0):
    _, tile = place()
    barrier = pltpu.get_barrier_semaphore()
    if not halos:
        pl.semaphore_wait(barrier, 2 * (NZ - 1) + more)
        return

    @pl.when(is_rim(tile))
    def _():
        pl.semaphore_wait(barrier, 2 * (NZ - 1) + 2 + SLOTS - 1)

    @pl.when(~is_rim(tile))
    def _():
        pl.semaphore_wait(barrier, 2 * (NZ - 1) + 2)


def sum_start(line, own, buf, send, recv):
    face, tile = place()

    @pl.loop(1, NZ)
    def _(step):
        mine, other, device = line(face, tile, step)
        remote(own, buf.at[mine], send.at[other], recv.at[mine], *device).start()

    mine, _, _ = line(face, tile, 0)
    buf[mine] = own[...]


def sum_finish(line, own, buf, send, recv):
    face, tile = place()

    @pl.loop(1, NZ)
    def _(step):
        _, other, device = line(face, tile, step)
        copy = remote(own, buf.at[other], send.at[other], recv.at[other], *device)
        copy.wait_recv()
        copy.wait_send()

    total = buf[0]
    for i in range(1, NZ):
        total = total + buf[i]
    return total


SUM_SCRATCH = [
    pltpu.VMEM((8, C), F32),
    pltpu.VMEM((8, C), F32),
    pltpu.VMEM((NZ, 8, C), F32),
    pltpu.VMEM((NZ, 8, C), F32),
    DMA((NZ,)),
    DMA((NZ,)),
    DMA((NZ,)),
    DMA((NZ,)),
]


HALO_SCRATCH = [
    pltpu.VMEM((SLOTS, 16, C), BF),
    pltpu.VMEM((SLOTS, 16, 128), BF),
    pltpu.VMEM((SLOTS, 16, C), BF),
    pltpu.VMEM((SLOTS, 16, 128), BF),
    pltpu.VMEM((32, C), F32),
    pltpu.VMEM((32, C), BF),
    pltpu.VMEM((NF, 32, C), BF),
    DMA((4,)),
    DMA((4,)),
    DMA((SLOTS,)),
    DMA((SLOTS,)),
    DMA((SLOTS,)),
    DMA((SLOTS,)),
    DMA((SLOTS,)),
    DMA((SLOTS,)),
    DMA((SLOTS,)),
    DMA((SLOTS,)),
    DMA((NF,)),
    DMA((NF,)),
    DMA((4,)),
]


class Halo:
    def __init__(self, fine, coarse, outs, scratch, tables):
        self.fine, self.coarse = fine, coarse
        self.hf, self.hc, self.r2f, self.r2c, self.sides = outs
        (
            self.r1f,
            self.r1c,
            self.stf,
            self.stc,
            self.rows,
            self.srec,
            self.sall,
            self.hs,
            self.hr,
            self.f1s,
            self.f1r,
            self.c1s,
            self.c1r,
            self.f2s,
            self.f2r,
            self.c2s,
            self.c2r,
            self.ss,
            self.sr,
            self.own,
        ) = scratch
        self.nb, self.ed = tables
        self.face, self.tile = place()

    def rows_copies(self):
        up = lax.rem(self.tile + 1, NT)
        down = lax.rem(self.tile + NT - 1, NT)
        plan = (
            (self.fine.at[RD - 1], self.hf.at[0], up),
            (self.fine.at[0], self.hf.at[1], down),
            (self.coarse.at[RD // 2 - 1], self.hc.at[0], up),
            (self.coarse.at[0], self.hc.at[1], down),
        )
        return [
            remote(src, dst, self.hs.at[i], self.hr.at[i], self.face, to)
            for i, (src, dst, to) in enumerate(plan)
        ]

    def chunk(self, slot):
        fine_row = jnp.where(self.tile == 0, 0, RD - 1)
        coarse_row = jnp.where(self.tile == 0, 0, RD // 2 - 1)
        return (
            self.fine.at[fine_row, pl.ds(multiple(slot, 16), 16), :],
            self.coarse.at[
                coarse_row,
                pl.ds(multiple(lax.div(slot, 2), 16), 16),
                pl.ds(multiple(lax.rem(slot, 2), 128), 128),
            ],
        )

    def landing(self, slot):
        return (
            self.r2f.at[pl.ds(multiple(slot, 16), 16), :],
            self.r2c.at[
                pl.ds(multiple(lax.div(slot, 2), 16), 16),
                pl.ds(multiple(lax.rem(slot, 2), 128), 128),
            ],
        )

    def hop1(self, step):
        mine = my_slot(self.face, self.tile)
        other = lax.rem(mine + step, SLOTS)
        device = slot_device(other)
        src_f, src_c = self.chunk(other)
        return (
            remote(src_f, self.r1f.at[mine], self.f1s.at[other], self.f1r.at[mine], *device),
            remote(src_c, self.r1c.at[mine], self.c1s.at[other], self.c1r.at[mine], *device),
        )

    def hop1_wait(self, step):
        mine = my_slot(self.face, self.tile)
        other = lax.rem(mine + step, SLOTS)
        device = slot_device(other)
        src_f, src_c = self.chunk(other)
        for copy in (
            remote(src_f, self.r1f.at[other], self.f1s.at[other], self.f1r.at[other], *device),
            remote(src_c, self.r1c.at[other], self.c1s.at[other], self.c1r.at[other], *device),
        ):
            copy.wait_recv()
            copy.wait_send()

    def hop2(self, step):
        mine = my_slot(self.face, self.tile)
        other = lax.rem(mine + step, SLOTS)
        device = slot_device(other)
        dst_f, dst_c = self.landing(mine)
        return (
            remote(self.stf.at[other], dst_f, self.f2s.at[other], self.f2r.at[mine], *device),
            remote(self.stc.at[other], dst_c, self.c2s.at[other], self.c2r.at[mine], *device),
        )

    def hop2_wait(self, step):
        mine = my_slot(self.face, self.tile)
        other = lax.rem(mine + step, SLOTS)
        device = slot_device(other)
        dst_f, dst_c = self.landing(other)
        for copy in (
            remote(self.stf.at[other], dst_f, self.f2s.at[other], self.f2r.at[other], *device),
            remote(self.stc.at[other], dst_c, self.c2s.at[other], self.c2r.at[other], *device),
        ):
            copy.wait_recv()
            copy.wait_send()

    def start(self):
        for copy in self.rows_copies():
            copy.start()

        @pl.when(is_rim(self.tile))
        def _():
            @pl.loop(1, SLOTS)
            def _(step):
                for copy in self.hop1(step):
                    copy.start()

            mine = my_slot(self.face, self.tile)
            src_f, src_c = self.chunk(mine)
            keep = (
                pltpu.make_async_copy(src_f, self.r1f.at[mine], self.own.at[0]),
                pltpu.make_async_copy(src_c, self.r1c.at[mine], self.own.at[1]),
            )
            for copy in keep:
                copy.start()
            for copy in keep:
                copy.wait()

    def middle(self):
        for copy in self.rows_copies():
            copy.wait_recv()
            copy.wait_send()
        fine_rows = [self.hf.at[0]] + [self.fine.at[r] for r in range(RD)] + [self.hf.at[1]]
        coarse_rows = [self.hc.at[0]] + [self.coarse.at[r] for r in range(RD // 2)]
        coarse_rows += [self.hc.at[1]]
        for i, row in enumerate(fine_rows + coarse_rows):
            side = row.shape[0]
            self.rows[i : i + 1, :] = row[0:16, :].astype(F32)[0:1]
            self.rows[16 + i : 17 + i, :] = row[side - 16 : side, :].astype(F32)[15:16]
        self.srec[...] = self.rows[...].astype(BF)

        @pl.loop(1, NF)
        def _(step):
            other = lax.rem(self.face + step, NF)
            remote(
                self.srec,
                self.sall.at[self.face],
                self.ss.at[other],
                self.sr.at[self.face],
                other,
                self.tile,
            ).start()

        self.sall[self.face] = self.srec[...]

        @pl.when(is_rim(self.tile))
        def _():
            mine = my_slot(self.face, self.tile)

            @pl.loop(1, SLOTS)
            def _(step):
                self.hop1_wait(step)

            @pl.loop(0, SLOTS)
            def _(slot):
                face, edge = lax.div(slot, 2), 2 * lax.rem(slot, 2)
                source = 2 * self.nb[face, edge] + lax.div(self.ed[face, edge], 2)
                self.stf[slot] = self.r1f[source]
                self.stc[slot] = self.r1c[source]

            @pl.loop(1, SLOTS)
            def _(step):
                for copy in self.hop2(step):
                    copy.start()

            dst_f, dst_c = self.landing(mine)
            keep = (
                pltpu.make_async_copy(self.stf.at[mine], dst_f, self.own.at[2]),
                pltpu.make_async_copy(self.stc.at[mine], dst_c, self.own.at[3]),
            )
            for copy in keep:
                copy.start()
            for copy in keep:
                copy.wait()

    def finish(self):
        @pl.loop(1, NF)
        def _(step):
            other = lax.rem(self.face + step, NF)
            copy = remote(
                self.srec,
                self.sall.at[other],
                self.ss.at[other],
                self.sr.at[other],
                other,
                self.tile,
            )
            copy.wait_recv()
            copy.wait_send()

        left_face, right_face = self.nb[self.face, 3], self.nb[self.face, 1]
        self.sides[0:16, :] = self.sall[left_face, 16:32, :]
        self.sides[16:32, :] = self.sall[right_face, 0:16, :]

        @pl.when(is_rim(self.tile))
        def _():
            @pl.loop(1, SLOTS)
            def _(step):
                self.hop2_wait(step)


HALO_OUTS = [
    jax.ShapeDtypeStruct((2, FS, C), BF),
    jax.ShapeDtypeStruct((2, CS, C), BF),
    jax.ShapeDtypeStruct((FS, C), BF),
    jax.ShapeDtypeStruct((CS, C), BF),
    jax.ShapeDtypeStruct((32, C), BF),
]


def iota(shape, dim):
    return lax.broadcasted_iota(jnp.int32, shape, dim)


def dot(a, b):
    return jnp.dot(a, b, preferred_element_type=F32)


def sigmoid(values):
    return 0.5 * jnp.tanh(0.5 * values) + 0.5


def pool_matrix():
    row, col = iota((CS, 2 * FS), 0), iota((CS, 2 * FS), 1)
    return jnp.where(lax.div(lax.rem(col, FS), 2) == row, 1.0, 0.0).astype(BF)


def spread_matrix():
    row, col = iota((FS, 2 * CS), 0), iota((FS, 2 * CS), 1)
    return jnp.where(lax.rem(col, CS) == lax.div(row, 2), 1.0, 0.0).astype(BF)


def spread(matrix, values):
    high = values.astype(BF)
    low = (values - high.astype(F32)).astype(BF)
    return dot(matrix, jnp.concatenate([high, low], axis=0))


def rim_matrix(side, flip):
    row, col = iota((side, side), 0), iota((side, side), 1)
    source = jnp.where(flip, side - 1 - row, row)
    return jnp.where(col == source, 1.0, 0.0).astype(BF)


def store_shifted(ref, row, values, left, right):
    n = values.shape[0]
    position = iota(values.shape, 0)
    before = jnp.where(position == 0, left, pltpu.roll(values, 1, 0))
    after = jnp.where(position == n - 1, right, pltpu.roll(values, n - 1, 0))
    ref[row, :, 0:C] = before.astype(BF)
    ref[row, :, C : 2 * C] = values.astype(BF)
    ref[row, :, 2 * C : 3 * C] = after.astype(BF)


def group_sum(values):
    lane = iota(values.shape, 1)
    for width in (1, 2, 4):
        up = pltpu.roll(values, width, 1)
        down = pltpu.roll(values, C - width, 1)
        values = values + jnp.where(lax.rem(lax.div(lane, width), 2) == 0, down, up)
    return values


def norm_vectors(total):
    grouped = group_sum(total) / (CELLS * GROUP)
    mean, second = grouped[0:1], grouped[1:2]
    return mean, lax.rsqrt(second - mean * mean + 1e-05)


def edge_flags(ed_ref):
    face, tile = place()
    first, last = tile == 0, tile == NT - 1
    flip_top = first & (ed_ref[face, 0] != 2)
    flip_bottom = last & (ed_ref[face, 2] != 0)
    return first, last, flip_top, flip_bottom


def masked_sides(sides, first, last):
    row = lax.rem(iota(sides.shape, 0), 16)
    top = (row == 0) | (row == RD + 2)
    bottom = (row == RD + 1) | (row == 15)
    zero = (top & first) | (bottom & last)
    return jnp.where(zero, 0.0, sides)


def halo_row(halo, rim, edge, at_rim, flip):
    side = halo.shape[1]
    across = dot(rim_matrix(side, flip), rim[...])
    return jnp.where(at_rim, across, halo[edge].astype(F32))


def back_weights(w_ref, out_ref):
    for k in range(3):
        for m in range(3):
            tap = w_ref[8 - (3 * k + m)].astype(F32)
            out_ref[k, m * C : (m + 1) * C, :] = tap.T.astype(BF)


def halo_weights(wt_ref, flip_top, flip_bottom):
    def turned(k):
        return jnp.concatenate(
            [wt_ref[k, (2 - m) * C : (3 - m) * C, :] for m in range(3)], axis=0
        )

    top = jnp.where(flip_top, turned(2), wt_ref[0])
    bottom = jnp.where(flip_bottom, turned(0), wt_ref[2])
    return top, bottom


def rows_of(ref, start, count):
    _, side, width = ref.shape
    return ref[pl.ds(start, count)].reshape(count * side, width)


def first_kernel(
    feat, cot, wf, wc, nb, ed, hf, hc, r2f, r2c, sides, gco, total, wtf, wtc, *scratch
):
    own_a, own_b, buf_a, buf_b, sa, ra, sb, rb = scratch[:8]
    halo = Halo(feat, gco, (hf, hc, r2f, r2c, sides), scratch[8:], (nb, ed))
    barrier_signal(True)

    matrix = pool_matrix()
    own_a[...] = jnp.zeros_like(own_a)

    @pl.loop(0, RD // 2)
    def _(i):
        gco[i] = dot(matrix, rows_of(cot, 2 * i, 2)).astype(BF)
        values = rows_of(feat, 2 * i, 2).astype(F32)
        own_a[0:1, :] += jnp.sum(values, axis=0, keepdims=True)
        own_a[1:2, :] += jnp.sum(values * values, axis=0, keepdims=True)

    barrier_wait(True)
    sum_start(line_a, own_a, buf_a, sa, ra)
    halo.start()
    back_weights(wc, wtc)
    own_b[...] = sum_finish(line_a, own_a, buf_a, sa, ra)
    sum_start(line_b, own_b, buf_b, sb, rb)
    halo.middle()
    back_weights(wf, wtf)
    total[...] = sum_finish(line_b, own_b, buf_b, sb, rb)
    halo.finish()


def forward_kernel(
    feat, cot, wf, wtc, gain, ed, hf, hc, r2f, r2c, sides, gco, total,
    x3, fine, coarse_in, grad_fine, u3, gci
):
    first, last, flip_top, flip_bottom = edge_flags(ed)
    mean, inverse = norm_vectors(total[...])
    scale = gain[...]

    def hidden(raw):
        act = (raw - mean) * inverse * scale
        return act * sigmoid(act)

    edge = sides[...].astype(F32)
    edge_hidden = masked_sides(hidden(edge), first, last)
    edge_coarse = masked_sides(edge, first, last)

    def put(i, raw):
        store_shifted(
            x3, i, hidden(raw).astype(BF).astype(F32), edge_hidden[i : i + 1],
            edge_hidden[16 + i : 17 + i],
        )

    put(0, halo_row(hf, r2f, 0, first, flip_top))
    for r in range(RD):
        put(r + 1, feat[r].astype(F32))
    put(RD + 1, halo_row(hf, r2f, 1, last, flip_bottom))

    half = RD // 2
    for i in range(half + 2):
        if i == 0:
            row = halo_row(hc, r2c, 0, first, flip_top)
        elif i == half + 1:
            row = halo_row(hc, r2c, 1, last, flip_bottom)
        else:
            row = gco[i - 1].astype(F32)
        j = RD + 2 + i
        store_shifted(u3, i, row, edge_coarse[j : j + 1], edge_coarse[16 + j : 17 + j])
    top, bottom = halo_weights(wtc, flip_top, flip_bottom)
    gci[...] = dot(rows_of(u3, 1, half), wtc[1]).reshape(half, CS, C)
    gci[1:half] += dot(rows_of(u3, 1, half - 1), wtc[0]).reshape(half - 1, CS, C)
    gci[0 : half - 1] += dot(rows_of(u3, 2, half - 1), wtc[2]).reshape(half - 1, CS, C)
    gci[0] += dot(u3[0], top)
    gci[half - 1] += dot(u3[half + 1], bottom)

    pool, widen = pool_matrix(), spread_matrix()

    @pl.loop(0, half)
    def _(i):
        total = dot(rows_of(x3, 2 * i, 2), wf[0])
        total += dot(rows_of(x3, 2 * i + 1, 2), wf[1])
        total += dot(rows_of(x3, 2 * i + 2, 2), wf[2])
        out = total.astype(BF)
        fine[pl.ds(2 * i, 2)] = out.reshape(2, FS, C)
        pooled = 0.25 * dot(pool, out)
        gate = sigmoid(pooled)
        coarse_in[i] = (pooled * gate).astype(BF)
        slope = gate * (1.0 + pooled * (1.0 - gate))
        wide = spread(widen, gci[i] * slope * 0.25)
        for r in range(2):
            grad_fine[2 * i + r] = (cot[2 * i + r].astype(F32) + wide).astype(BF)


def second_kernel(
    grad_fine, coarse_in, nb, ed, hf, hc, r2f, r2c, sides, *scratch
):
    halo = Halo(grad_fine, coarse_in, (hf, hc, r2f, r2c, sides), scratch, (nb, ed))
    barrier_signal(True)
    barrier_wait(True)
    halo.start()
    halo.middle()
    halo.finish()


def backward_kernel(
    feat, x3, fine, coarse_in, grad_fine, gco, wc, wtf, gain, total, ed,
    hf, hc, r2f, r2c, sides, output, ga, sums, shares, c3, u3, gt, gct
):
    first, last, flip_top, flip_bottom = edge_flags(ed)
    mean, inverse = norm_vectors(total[...])
    scale = gain[...]
    half = RD // 2
    edge = masked_sides(sides[...].astype(F32), first, last)

    for i in range(half + 2):
        if i == 0:
            row = halo_row(hc, r2c, 0, first, flip_top)
        elif i == half + 1:
            row = halo_row(hc, r2c, 1, last, flip_bottom)
        else:
            row = coarse_in[i - 1].astype(F32)
        j = RD + 2 + i
        store_shifted(c3, i, row, edge[j : j + 1], edge[16 + j : 17 + j])

    for i in range(RD + 2):
        if i == 0:
            row = halo_row(hf, r2f, 0, first, flip_top)
        elif i == RD + 1:
            row = halo_row(hf, r2f, 1, last, flip_bottom)
        else:
            row = grad_fine[i - 1].astype(F32)
        store_shifted(u3, i, row, edge[i : i + 1], edge[16 + i : 17 + i])

    for r in range(RD):
        gt[:, r * FS : (r + 1) * FS] = grad_fine[r].astype(F32).T.astype(BF)
    for r in range(half):
        gct[:, r * CS : (r + 1) * CS] = gco[r].astype(F32).T.astype(BF)
    for k in range(3):
        fine_part = dot(gt[...], rows_of(x3, k, RD))
        coarse_part = dot(gct[...], rows_of(c3, k, half))
        for m in range(3):
            tap = 3 * k + m
            pair = [
                part[:, m * C : (m + 1) * C].T.reshape(NT, 8, C)
                for part in (fine_part, coarse_part)
            ]
            shares[:, 16 * tap : 16 * tap + 16, :] = jnp.concatenate(pair, axis=1).astype(BF)

    widen = spread_matrix()

    @pl.loop(0, half)
    def _(i):
        out = dot(c3[i], wc[0]) + dot(c3[i + 1], wc[1]) + dot(c3[i + 2], wc[2])
        wide = spread(widen, out)
        for r in range(2):
            output[2 * i + r] = (fine[2 * i + r].astype(F32) + wide).astype(BF)

    top, bottom = halo_weights(wtf, flip_top, flip_bottom)
    ga[1 : RD - 1] = jnp.zeros((RD - 2, FS, C), F32)
    ga[0] = dot(u3[0], top)
    ga[RD - 1] = dot(u3[RD + 1], bottom)
    u3[0] = jnp.zeros_like(u3[0])
    u3[RD + 1] = jnp.zeros_like(u3[0])
    sums[...] = jnp.zeros_like(sums)

    @pl.loop(0, half)
    def _(i):
        grad = dot(rows_of(u3, 2 * i, 2), wtf[0])
        grad += dot(rows_of(u3, 2 * i + 1, 2), wtf[1])
        grad += dot(rows_of(u3, 2 * i + 2, 2), wtf[2])
        grad += rows_of(ga, 2 * i, 2)
        normed = (rows_of(feat, 2 * i, 2).astype(F32) - mean) * inverse
        act = normed * scale
        gate = sigmoid(act)
        grad = grad * (gate * (1.0 + act * (1.0 - gate)))
        ga[pl.ds(2 * i, 2)] = grad.reshape(2, FS, C)
        sums[0:1, :] += jnp.sum(grad * normed, axis=0, keepdims=True)
        sums[1:2, :] += jnp.sum(grad, axis=0, keepdims=True)


UNITS = 144


def reduce_kernel(
    shares, sums, grads, total, own_a, own_b, buf_a, buf_b, sa, ra, sb, rb,
    r0, part, r1, block, r2, s0, q0, s1, q1, s2, q2
):
    face, tile = place()
    core, chip = lax.rem(tile, 2), lax.div(tile, 2)
    sibling = tile + 1 - 2 * core
    barrier = pltpu.get_barrier_semaphore()
    barrier_signal(False)

    far = lax.rem(tile + NZ, NT)
    far_base = far - lax.rem(far, NZ)

    @pl.loop(0, NZ // 2)
    def _(z):
        signal(barrier, face, far_base + 2 * z + core)

    own_a[...] = sums[...]
    barrier_wait(False, NZ // 2)

    def swap(q):
        return remote(
            shares.at[pl.ds(4 * q, 4), 1 - core],
            r0.at[pl.ds(4 * q, 4)],
            s0.at[q],
            q0.at[q],
            face,
            sibling,
        )

    for q in range(4):
        swap(q).start()
    sum_start(line_a, own_a, buf_a, sa, ra)

    def scatter(other, slot):
        return remote(
            part.at[other], r1.at[slot], s1.at[other], q1.at[slot], face, 2 * other + core
        )

    for q in range(4):
        swap(q).wait_recv()

        @pl.loop(4 * q, 4 * q + 4)
        def _(j):
            both = shares[j, core].astype(F32) + r0[j].astype(F32)
            part[j] = both.astype(BF)

            @pl.when(j != chip)
            def _():
                scatter(j, chip).start()

    own_b[...] = sum_finish(line_a, own_a, buf_a, sa, ra)
    sum_start(line_b, own_b, buf_b, sb, rb)
    r1[chip] = part[chip]

    @pl.loop(1, 16)
    def _(step):
        other = lax.rem(chip + step, 16)
        scatter(other, other).wait_recv()

    acc = r1[0].astype(F32)
    for j in range(1, 16):
        acc = acc + r1[j].astype(F32)
    block[...] = acc.astype(BF)

    def share(other, slot):
        return remote(block, r2.at[slot], s2.at[other], q2.at[slot], other, tile)

    @pl.loop(1, NF)
    def _(step):
        share(lax.rem(face + step, NF), face).start()

    r2[face] = block[...]
    total[...] = sum_finish(line_b, own_b, buf_b, sb, rb)

    @pl.loop(1, NF)
    def _(step):
        other = lax.rem(face + step, NF)
        share(other, other).wait_recv()

    acc = r2[0].astype(F32)
    for j in range(1, NF):
        acc = acc + r2[j].astype(F32)
    grads[...] = acc * (1.0 / CELLS)

    for q in range(4):
        swap(q).wait_send()

    @pl.loop(1, 16)
    def _(step):
        other = lax.rem(chip + step, 16)
        scatter(other, other).wait_send()

    @pl.loop(1, NF)
    def _(step):
        other = lax.rem(face + step, NF)
        share(other, other).wait_send()


def last_kernel(feat, ga, gain, total, sums, grad_features, grad_gain):
    mean, inverse = norm_vectors(total[...])
    scale = gain[...]
    slope_sum, shift_sum = sums[0:1], sums[1:2]
    grad_gain[...] = slope_sum / CELLS
    row = iota((8, C), 0)
    weighted = sums[...] * scale
    grouped = group_sum(weighted) / (CELLS * GROUP)
    group_slope, group_shift = grouped[0:1], grouped[1:2]
    normed = (feat[0].astype(F32) - mean) * inverse
    grad_features[0] = inverse * (scale * ga[0] - group_shift - normed * group_slope)


def shape(dims, dtype):
    return jax.ShapeDtypeStruct(dims, dtype)


def call(kernel, ins, outs, scratch, collective=None, **more):
    params = {"vmem_limit_bytes": VMEM_LIMIT}
    if collective is not None:
        params.update(collective_id=collective, has_side_effects=True)
    return pl.pallas_call(
        kernel,
        in_specs=ins,
        out_specs=[VM] * len(outs),
        out_shape=outs,
        scratch_shapes=scratch,
        compiler_params=pltpu.CompilerParams(**params),
        **more,
    )


def on_device(features, cotangent, w_fine, w_coarse, gain, neighbors, neighbor_edges):
    feat, cot = features[0], cotangent[0]
    half = RD // 2
    gain_row = gain[None]
    w_fine_rows = w_fine.reshape(3, 3 * C, C)
    w_coarse_rows = w_coarse.reshape(3, 3 * C, C)

    hf, hc, r2f, r2c, sides, gco, total, wtf, wtc = call(
        first_kernel,
        [VM] * 4 + [SM] * 2,
        HALO_OUTS
        + [
            shape((half, CS, C), BF),
            shape((8, C), F32),
            shape((3, 3 * C, C), BF),
            shape((3, 3 * C, C), BF),
        ],
        SUM_SCRATCH + HALO_SCRATCH,
        collective=1,
    )(feat, cot, w_fine, w_coarse, neighbors, neighbor_edges)

    x3, fine, coarse_in, grad_fine = call(
        forward_kernel,
        [VM] * 5 + [SM] + [VM] * 7,
        [
            shape((RD + 2, FS, 3 * C), BF),
            shape((RD, FS, C), BF),
            shape((half, CS, C), BF),
            shape((RD, FS, C), BF),
        ],
        [pltpu.VMEM((half + 2, CS, 3 * C), BF), pltpu.VMEM((half, CS, C), F32)],
    )(
        feat, cot, w_fine_rows, wtc, gain_row, neighbor_edges,
        hf, hc, r2f, r2c, sides, gco, total,
    )

    hf2, hc2, r2f2, r2c2, sides2 = call(
        second_kernel, [VM] * 2 + [SM] * 2, HALO_OUTS, HALO_SCRATCH, collective=2
    )(grad_fine, coarse_in, neighbors, neighbor_edges)

    output, ga, sums, shares = call(
        backward_kernel,
        [VM] * 10 + [SM] + [VM] * 5,
        [
            shape((RD, FS, C), BF),
            shape((RD, FS, C), F32),
            shape((8, C), F32),
            shape((NT, UNITS, C), BF),
        ],
        [
            pltpu.VMEM((half + 2, CS, 3 * C), BF),
            pltpu.VMEM((RD + 2, FS, 3 * C), BF),
            pltpu.VMEM((C, RD * FS), BF),
            pltpu.VMEM((C, half * CS), BF),
        ],
    )(
        feat, x3, fine, coarse_in, grad_fine, gco, w_coarse_rows, wtf, gain_row, total,
        neighbor_edges, hf2, hc2, r2f2, r2c2, sides2,
    )

    grads, all_sums = call(
        reduce_kernel,
        [VM] * 2,
        [shape((UNITS, C), F32), shape((8, C), F32)],
        SUM_SCRATCH
        + [
            pltpu.VMEM((16, UNITS, C), BF),
            pltpu.VMEM((16, UNITS, C), BF),
            pltpu.VMEM((16, UNITS, C), BF),
            pltpu.VMEM((UNITS, C), BF),
            pltpu.VMEM((NF, UNITS, C), BF),
            DMA((4,)),
            DMA((4,)),
            DMA((16,)),
            DMA((16,)),
            DMA((NF,)),
            DMA((NF,)),
        ],
        collective=3,
    )(shares.reshape(16, 2, UNITS, C), sums)

    row = pl.BlockSpec((1, FS, C), lambda i: (i, 0, 0))
    vector = pl.BlockSpec((1, C), lambda i: (0, 0))
    block = pl.BlockSpec((8, C), lambda i: (0, 0))
    grad_features, grad_gain = pl.pallas_call(
        last_kernel,
        grid=(RD,),
        in_specs=[row, row, vector, block, block],
        out_specs=[row, vector],
        out_shape=[shape((RD, FS, C), F32), shape((1, C), F32)],
        compiler_params=pltpu.CompilerParams(vmem_limit_bytes=VMEM_LIMIT),
    )(feat, ga, gain_row, total, all_sums)

    grads = grads.reshape(9, 2, 8, C)
    return (output[None], grad_features[None], grads[:, 0], grads[:, 1], grad_gain[0])


def solution(mesh):
    return jax.shard_map(
        on_device,
        mesh=mesh,
        in_specs=(
            P("face", "tile", None, None),
            P("face", "tile", None, None),
            P(),
            P(),
            P(),
            P(),
            P(),
        ),
        out_specs=(
            P("face", "tile", None, None),
            P("face", "tile", None, None),
            P(None, "tile", None),
            P(None, "tile", None),
            P(),
        ),
        check_vma=False,
    )
```

time: 712 us -> 144 us (0.20)
  the two profiles are of different devices: /device:TPU:4 before, /device:TPU:248 now
where the time goes in v1:
time: 144 us
  Pallas kernels  140 us (97%)
  local copies, waits for them, and re-layouts  3.36 us (2%)
    pallas_call x1, Pallas kernels, on_device(): call(reduce_kernel, [VM] * 2, [shape((UNITS, C), F32), shape((8, C), F32)...  65 us
    pallas_call x1, Pallas kernels, on_device(): call(first_kernel, [VM] * 4 + [SM] * 2, HALO_OUTS + [shape((half, CS, C),...  21.8 us
    pallas_call x1, Pallas kernels, on_device(): call(second_kernel, [VM] * 2 + [SM] * 2, HALO_OUTS, HALO_SCRATCH, collect...  18.5 us
    pallas_call x1, Pallas kernels, on_device(): call(backward_kernel, [VM] * 10 + [SM] + [VM] * 5, [shape((RD, FS, C), BF...  16.2 us
    pallas_call x1, Pallas kernels, on_device(): call(forward_kernel, [VM] * 5 + [SM] + [VM] * 7, [shape((RD + 2, FS, 3 *...  11.5 us
    pallas_call x1, Pallas kernels, on_device(): pl.pallas_call(last_kernel, grid=(RD,), in_specs=[row, row, vector, block...  7.07 us

profile of v1, /device:TPU:248, one launch (start us, length us, event | category | flops | bytes accessed | tf_op | source)
XLA Modules:
  0.0 144.0 jit_solution(2798867376882226621)
XLA Ops:
  0.6 1.3 copy.13.ed
  2.0 1.3 copy.12.nb
  3.3 21.8 %shard_map.110 = (bf16[2,256,256]{2,1,0:T(8,128)(2,1)}, bf16[2,128,256]{2,1,0:T(8,128)(2,1)}, bf16[256,256]{1,0:T(8,128)(2,1)}, bf16[128,256]{1,0:T(8,128)(2,1)}...) custom-call(bf16[8,256,256]{2,1,0:T(8,128)(2,1)} %bitcast.18, ...), custom_call_target="tpu_custom_call" | custom-call | tf_op jit(solution)/shard_map/pallas_call | solution.py:825
  25.2 11.5 %shard_map.111 = (bf16[10,256,768]{2,1,0:T(8,128)(2,1)}, bf16[8,256,256]{2,1,0:T(8,128)(2,1)}, bf16[4,128,256]{2,1,0:T(8,128)(2,1)}, bf16[8,256,256]{2,1,0:T(8,128)(2,1)}) custom-call(bf16[8,256,256]{2,1,0:T(8,128)(2,1)} %bitcast.19, bf16[8,256,256]{2,1,0:T(8,128)(2,1)} %bitcast.25, bf16[3,768,256]{2,1,0:T(8,128)(2,1)} %bitcast.23, ...), custom_call_target="tpu_custom_call" | custom-call | tf_op jit(solution)/shard_map/pallas_call | solution.py:839
  36.7 18.5 %shard_map.112 = (bf16[2,256,256]{2,1,0:T(8,128)(2,1)}, bf16[2,128,256]{2,1,0:T(8,128)(2,1)}, bf16[256,256]{1,0:T(8,128)(2,1)}, bf16[128,256]{1,0:T(8,128)(2,1)}, bf16[32,256]{1,0:T(8,128)(2,1)}) custom-call(bf16[8,256,256]{2,1,0:T(8,128)(2,1)} %get-tuple-element.42.grad_fine, bf16[4,128,256]{2,1,0:T(8,128)(2,1)} %get-tuple-element.41.coarse_in, ...), custom_call_target="tpu_custom_call" | custom-call | tf_op jit(solution)/shard_map/pallas_call | solution.py:854
  55.1 16.2 %shard_map.113 = (bf16[8,256,256]{2,1,0:T(8,128)(2,1)}, f32[8,256,256]{2,1,0:T(8,128)}, f32[8,256]{1,0:T(8,128)}, bf16[32,144,256]{2,1,0:T(8,128)(2,1)}) custom-call(bf16[8,256,256]{2,1,0:T(8,128)(2,1)} %bitcast.20, bf16[10,256,768]{2,1,0:T(8,128)(2,1)} %get-tuple-element.39.x3, bf16[8,256,256]{2,1,0:T(8,128)(2,1)} %get-tuple-element.40.fine, ...), custom_call_target="tpu_custom_call" | custom-call | tf_op jit(solution)/shard_map/pallas_call | solution.py:858
  71.3 65.0 %shard_map.114 = (f32[144,256]{1,0:T(8,128)}, f32[8,256]{1,0:T(8,128)}) custom-call(bf16[16,2,144,256]{3,2,1,0:T(8,128)(2,1)} %bitcast.26, f32[8,256]{1,0:T(8,128)} %get-tuple-element.52.sums), custom_call_target="tpu_custom_call" | custom-call | tf_op jit(solution)/shard_map/pallas_call | solution.py:878
  136.3 0.0 copy-start
  136.3 7.1 %shard_map.115 = (f32[8,256,256]{2,1,0:T(8,128)}, f32[1,256]{1,0:T(1,128)}) custom-call(bf16[8,256,256]{2,1,0:T(8,128)(2,1)} %bitcast.21, f32[8,256,256]{2,1,0:T(8,128)} %get-tuple-element.50.ga, f32[1,256]{1,0:T(1,128)} %bitcast.30, f32[8,256]{1,0:T(8,128)} %get-tuple-element.38.total, f32[8,256]{1,0:T(8,128)} %get-tuple-element.53.sums), custom_call_target="tpu_custom_call" | custom-call | tf_op jit(solution)/shard_map/pallas_call | solution.py:902
  143.4 0.0 copy-done
  143.4 0.7 slice_bitcast_fusion
Async XLA Ops:
  136.3 7.1 %copy-start = (f32[144,256]{1,0:T(8,128)S(1)}, f32[144,256]{1,0:T(8,128)}, u32[]{:S(2)}) copy-start(f32[144,256]{1,0:T(8,128)} %get-tuple-element.55) | copy-start | bytes 442372

commit v2 on v1

v2 whole, which is shorter than its diff:
```python
import jax
import jax.numpy as jnp
from jax import lax
from jax.experimental import pallas as pl
from jax.experimental.pallas import tpu as pltpu
from jax.sharding import PartitionSpec as P

BF = jnp.bfloat16
F32 = jnp.float32
MESH = pl.DeviceIdType.MESH
NF = 8
NT = 32
NZ = 16
RD = 8
FS = 256
CS = 128
C = 256
GROUP = 8
SLOTS = 16
CELLS = NF * FS * FS
VMEM_LIMIT = 60 * 1024 * 1024

VM = pl.BlockSpec(memory_space=pltpu.VMEM)
SM = pl.BlockSpec(memory_space=pltpu.SMEM)
DMA = pltpu.SemaphoreType.DMA


def remote(src, dst, send, recv, face, tile):
    return pltpu.make_async_remote_copy(
        src_ref=src,
        dst_ref=dst,
        send_sem=send,
        recv_sem=recv,
        device_id=(face, tile),
        device_id_type=MESH,
    )


def place():
    return lax.axis_index("face"), lax.axis_index("tile")


def is_rim(tile):
    return (tile == 0) | (tile == NT - 1)


def slot_device(slot):
    return lax.div(slot, 2), (NT - 1) * lax.rem(slot, 2)


def my_slot(face, tile):
    return 2 * face + jnp.where(tile == NT - 1, 1, 0)


def multiple(value, of):
    return pl.multiple_of(value * of, of)


def signal(barrier, face, tile):
    pl.semaphore_signal(barrier, inc=1, device_id=(face, tile), device_id_type=MESH)


def line_a(face, tile, step):
    mine = lax.rem(tile, NZ)
    other = lax.rem(mine + step, NZ)
    return mine, other, (face, tile - mine + other)


def line_b(face, tile, step):
    mine = face * 2 + lax.div(tile, NZ)
    other = lax.rem(mine + step, 2 * NF)
    return mine, other, (lax.div(other, 2), lax.rem(other, 2) * NZ + lax.rem(tile, NZ))


def barrier_signal():
    face, tile = place()
    barrier = pltpu.get_barrier_semaphore()
    across = lax.rem(tile + NZ, NT)
    across = across - lax.rem(across, NZ) + lax.rem(tile, 2)

    @pl.loop(1, NZ)
    def _(step):
        for line in (line_a, line_b):
            _, _, device = line(face, tile, step)
            signal(barrier, *device)

    @pl.loop(0, NZ // 2)
    def _(z):
        signal(barrier, face, across + 2 * z)

    signal(barrier, face, lax.rem(tile + 1, NT))
    signal(barrier, face, lax.rem(tile + NT - 1, NT))

    @pl.when(is_rim(tile))
    def _():
        mine = my_slot(face, tile)

        @pl.loop(1, SLOTS)
        def _(step):
            signal(barrier, *slot_device(lax.rem(mine + step, SLOTS)))


def barrier_wait():
    _, tile = place()
    barrier = pltpu.get_barrier_semaphore()
    count = 2 * (NZ - 1) + NZ // 2 + 2

    @pl.when(is_rim(tile))
    def _():
        pl.semaphore_wait(barrier, count + SLOTS - 1)

    @pl.when(~is_rim(tile))
    def _():
        pl.semaphore_wait(barrier, count)


def sum_start(line, own, buf, send, recv):
    face, tile = place()

    @pl.loop(1, NZ)
    def _(step):
        mine, other, device = line(face, tile, step)
        remote(own, buf.at[mine], send.at[other], recv.at[mine], *device).start()

    mine, _, _ = line(face, tile, 0)
    buf[mine] = own[...]


def sum_finish(line, own, buf, send, recv):
    face, tile = place()

    @pl.loop(1, NZ)
    def _(step):
        _, other, device = line(face, tile, step)
        copy = remote(own, buf.at[other], send.at[other], recv.at[other], *device)
        copy.wait_recv()
        copy.wait_send()

    total = buf[0]
    for i in range(1, NZ):
        total = total + buf[i]
    return total


SUM_SCRATCH = [
    pltpu.VMEM((8, C), F32),
    pltpu.VMEM((8, C), F32),
    pltpu.VMEM((NZ, 8, C), F32),
    pltpu.VMEM((NZ, 8, C), F32),
    DMA((NZ,)),
    DMA((NZ,)),
    DMA((NZ,)),
    DMA((NZ,)),
]


HALO_SCRATCH = [
    pltpu.VMEM((2, FS, C), BF),
    pltpu.VMEM((2, CS, C), BF),
    pltpu.VMEM((FS, C), BF),
    pltpu.VMEM((CS, C), BF),
    pltpu.VMEM((32, C), BF),
    pltpu.VMEM((SLOTS, 16, C), BF),
    pltpu.VMEM((SLOTS, 16, 128), BF),
    pltpu.VMEM((SLOTS, 16, C), BF),
    pltpu.VMEM((SLOTS, 16, 128), BF),
    pltpu.VMEM((32, C), F32),
    pltpu.VMEM((32, C), BF),
    pltpu.VMEM((NF, 32, C), BF),
    DMA((4,)),
    DMA((4,)),
    DMA((SLOTS,)),
    DMA((SLOTS,)),
    DMA((SLOTS,)),
    DMA((SLOTS,)),
    DMA((SLOTS,)),
    DMA((SLOTS,)),
    DMA((SLOTS,)),
    DMA((SLOTS,)),
    DMA((NF,)),
    DMA((NF,)),
    DMA((4,)),
]


class Halo:
    def __init__(self, fine, coarse, scratch, tables):
        self.fine, self.coarse = fine, coarse
        (
            self.hf,
            self.hc,
            self.r2f,
            self.r2c,
            self.sides,
            self.r1f,
            self.r1c,
            self.stf,
            self.stc,
            self.rows,
            self.srec,
            self.sall,
            self.hs,
            self.hr,
            self.f1s,
            self.f1r,
            self.c1s,
            self.c1r,
            self.f2s,
            self.f2r,
            self.c2s,
            self.c2r,
            self.ss,
            self.sr,
            self.own,
        ) = scratch
        self.nb, self.ed = tables
        self.face, self.tile = place()

    def rows_copies(self):
        up = lax.rem(self.tile + 1, NT)
        down = lax.rem(self.tile + NT - 1, NT)
        plan = (
            (self.fine.at[RD - 1], self.hf.at[0], up),
            (self.fine.at[0], self.hf.at[1], down),
            (self.coarse.at[RD // 2 - 1], self.hc.at[0], up),
            (self.coarse.at[0], self.hc.at[1], down),
        )
        return [
            remote(src, dst, self.hs.at[i], self.hr.at[i], self.face, to)
            for i, (src, dst, to) in enumerate(plan)
        ]

    def chunk(self, slot):
        fine_row = jnp.where(self.tile == 0, 0, RD - 1)
        coarse_row = jnp.where(self.tile == 0, 0, RD // 2 - 1)
        return (
            self.fine.at[fine_row, pl.ds(multiple(slot, 16), 16), :],
            self.coarse.at[
                coarse_row,
                pl.ds(multiple(lax.div(slot, 2), 16), 16),
                pl.ds(multiple(lax.rem(slot, 2), 128), 128),
            ],
        )

    def landing(self, slot):
        return (
            self.r2f.at[pl.ds(multiple(slot, 16), 16), :],
            self.r2c.at[
                pl.ds(multiple(lax.div(slot, 2), 16), 16),
                pl.ds(multiple(lax.rem(slot, 2), 128), 128),
            ],
        )

    def hop1(self, step):
        mine = my_slot(self.face, self.tile)
        other = lax.rem(mine + step, SLOTS)
        device = slot_device(other)
        src_f, src_c = self.chunk(other)
        return (
            remote(src_f, self.r1f.at[mine], self.f1s.at[other], self.f1r.at[mine], *device),
            remote(src_c, self.r1c.at[mine], self.c1s.at[other], self.c1r.at[mine], *device),
        )

    def hop1_wait(self, step):
        mine = my_slot(self.face, self.tile)
        other = lax.rem(mine + step, SLOTS)
        device = slot_device(other)
        src_f, src_c = self.chunk(other)
        for copy in (
            remote(src_f, self.r1f.at[other], self.f1s.at[other], self.f1r.at[other], *device),
            remote(src_c, self.r1c.at[other], self.c1s.at[other], self.c1r.at[other], *device),
        ):
            copy.wait_recv()
            copy.wait_send()

    def hop2(self, step):
        mine = my_slot(self.face, self.tile)
        other = lax.rem(mine + step, SLOTS)
        device = slot_device(other)
        dst_f, dst_c = self.landing(mine)
        return (
            remote(self.stf.at[other], dst_f, self.f2s.at[other], self.f2r.at[mine], *device),
            remote(self.stc.at[other], dst_c, self.c2s.at[other], self.c2r.at[mine], *device),
        )

    def hop2_wait(self, step):
        mine = my_slot(self.face, self.tile)
        other = lax.rem(mine + step, SLOTS)
        device = slot_device(other)
        dst_f, dst_c = self.landing(other)
        for copy in (
            remote(self.stf.at[other], dst_f, self.f2s.at[other], self.f2r.at[other], *device),
            remote(self.stc.at[other], dst_c, self.c2s.at[other], self.c2r.at[other], *device),
        ):
            copy.wait_recv()
            copy.wait_send()

    def start(self):
        for copy in self.rows_copies():
            copy.start()

        @pl.when(is_rim(self.tile))
        def _():
            @pl.loop(1, SLOTS)
            def _(step):
                for copy in self.hop1(step):
                    copy.start()

            mine = my_slot(self.face, self.tile)
            src_f, src_c = self.chunk(mine)
            keep = (
                pltpu.make_async_copy(src_f, self.r1f.at[mine], self.own.at[0]),
                pltpu.make_async_copy(src_c, self.r1c.at[mine], self.own.at[1]),
            )
            for copy in keep:
                copy.start()
            for copy in keep:
                copy.wait()

    def middle(self):
        for copy in self.rows_copies():
            copy.wait_recv()
            copy.wait_send()
        fine_rows = [self.hf.at[0]] + [self.fine.at[r] for r in range(RD)] + [self.hf.at[1]]
        coarse_rows = [self.hc.at[0]] + [self.coarse.at[r] for r in range(RD // 2)]
        coarse_rows += [self.hc.at[1]]
        for i, row in enumerate(fine_rows + coarse_rows):
            side = row.shape[0]
            self.rows[i : i + 1, :] = row[0:16, :].astype(F32)[0:1]
            self.rows[16 + i : 17 + i, :] = row[side - 16 : side, :].astype(F32)[15:16]
        self.srec[...] = self.rows[...].astype(BF)

        @pl.loop(1, NF)
        def _(step):
            other = lax.rem(self.face + step, NF)
            remote(
                self.srec,
                self.sall.at[self.face],
                self.ss.at[other],
                self.sr.at[self.face],
                other,
                self.tile,
            ).start()

        self.sall[self.face] = self.srec[...]

        @pl.when(is_rim(self.tile))
        def _():
            mine = my_slot(self.face, self.tile)

            @pl.loop(1, SLOTS)
            def _(step):
                self.hop1_wait(step)

            @pl.loop(0, SLOTS)
            def _(slot):
                face, edge = lax.div(slot, 2), 2 * lax.rem(slot, 2)
                source = 2 * self.nb[face, edge] + lax.div(self.ed[face, edge], 2)
                self.stf[slot] = self.r1f[source]
                self.stc[slot] = self.r1c[source]

            @pl.loop(1, SLOTS)
            def _(step):
                for copy in self.hop2(step):
                    copy.start()

            dst_f, dst_c = self.landing(mine)
            keep = (
                pltpu.make_async_copy(self.stf.at[mine], dst_f, self.own.at[2]),
                pltpu.make_async_copy(self.stc.at[mine], dst_c, self.own.at[3]),
            )
            for copy in keep:
                copy.start()
            for copy in keep:
                copy.wait()

    def finish(self, flips):
        @pl.loop(1, NF)
        def _(step):
            other = lax.rem(self.face + step, NF)
            copy = remote(
                self.srec,
                self.sall.at[other],
                self.ss.at[other],
                self.sr.at[other],
                other,
                self.tile,
            )
            copy.wait_recv()
            copy.wait_send()

        left_face, right_face = self.nb[self.face, 3], self.nb[self.face, 1]
        self.sides[0:16, :] = self.sall[left_face, 16:32, :]
        self.sides[16:32, :] = self.sall[right_face, 0:16, :]

        @pl.when(is_rim(self.tile))
        def _():
            @pl.loop(1, SLOTS)
            def _(step):
                self.hop2_wait(step)

            flip_top, flip_bottom = flips
            flip = jnp.where(self.tile == 0, flip_top, flip_bottom)
            edge = jnp.where(self.tile == 0, 0, 1)
            self.hf[edge] = dot(rim_matrix(FS, flip), self.r2f[...]).astype(BF)
            self.hc[edge] = dot(rim_matrix(CS, flip), self.r2c[...]).astype(BF)


def iota(shape, dim):
    return lax.broadcasted_iota(jnp.int32, shape, dim)


def dot(a, b):
    return jnp.dot(a, b, preferred_element_type=F32)


def sigmoid(values):
    return 0.5 * jnp.tanh(0.5 * values) + 0.5


def pool_matrix():
    row, col = iota((CS, 2 * FS), 0), iota((CS, 2 * FS), 1)
    return jnp.where(lax.div(lax.rem(col, FS), 2) == row, 1.0, 0.0).astype(BF)


def spread_matrix():
    row, col = iota((FS, 2 * CS), 0), iota((FS, 2 * CS), 1)
    return jnp.where(lax.rem(col, CS) == lax.div(row, 2), 1.0, 0.0).astype(BF)


def spread(matrix, values):
    high = values.astype(BF)
    low = (values - high.astype(F32)).astype(BF)
    return dot(matrix, jnp.concatenate([high, low], axis=0))


def rim_matrix(side, flip):
    row, col = iota((side, side), 0), iota((side, side), 1)
    source = jnp.where(flip, side - 1 - row, row)
    return jnp.where(col == source, 1.0, 0.0).astype(BF)


def store_shifted(ref, row, values, left, right):
    n = values.shape[0]
    position = iota(values.shape, 0)
    before = jnp.where(position == 0, left, pltpu.roll(values, 1, 0))
    after = jnp.where(position == n - 1, right, pltpu.roll(values, n - 1, 0))
    ref[row, :, 0:C] = before.astype(BF)
    ref[row, :, C : 2 * C] = values.astype(BF)
    ref[row, :, 2 * C : 3 * C] = after.astype(BF)


def group_sum(values):
    lane = iota(values.shape, 1)
    for width in (1, 2, 4):
        up = pltpu.roll(values, width, 1)
        down = pltpu.roll(values, C - width, 1)
        values = values + jnp.where(lax.rem(lax.div(lane, width), 2) == 0, down, up)
    return values


def norm_vectors(total):
    grouped = group_sum(total) / (CELLS * GROUP)
    mean, second = grouped[0:1], grouped[1:2]
    return mean, lax.rsqrt(second - mean * mean + 1e-05)


def edge_flags(ed_ref):
    face, tile = place()
    first, last = tile == 0, tile == NT - 1
    flip_top = first & (ed_ref[face, 0] != 2)
    flip_bottom = last & (ed_ref[face, 2] != 0)
    return first, last, flip_top, flip_bottom


def masked_sides(sides, first, last):
    row = lax.rem(iota(sides.shape, 0), 16)
    top = (row == 0) | (row == RD + 2)
    bottom = (row == RD + 1) | (row == 15)
    zero = (top & first) | (bottom & last)
    return jnp.where(zero, 0.0, sides)


def back_weights(w_ref, out_ref):
    for k in range(3):
        for m in range(3):
            tap = w_ref[8 - (3 * k + m)].astype(F32)
            out_ref[k, m * C : (m + 1) * C, :] = tap.T.astype(BF)


def halo_weights(wt_ref, flip_top, flip_bottom):
    def turned(k):
        return jnp.concatenate(
            [wt_ref[k, (2 - m) * C : (3 - m) * C, :] for m in range(3)], axis=0
        )

    top = jnp.where(flip_top, turned(2), wt_ref[0])
    bottom = jnp.where(flip_bottom, turned(0), wt_ref[2])
    return top, bottom


def rows_of(ref, start, count):
    _, side, width = ref.shape
    return ref[pl.ds(start, count)].reshape(count * side, width)


def taps_of(ref, k):
    return ref[3 * k : 3 * k + 3].reshape(3 * C, C)


SHARE = 144
NC = 16


def put_share(shares, tap, product):
    turned = product.T.reshape(NC, 2, 8, C)
    halves = [turned[..., :128], turned[..., 128:]]
    shares[:, :, 16 * tap : 16 * tap + 16, :] = jnp.concatenate(halves, axis=2).astype(BF)


def put_grads(out, total):
    total = (total * (1.0 / CELLS)).reshape(9, 2, 8, 128)
    out[:, :, 0:128] = total[:, 0]
    out[:, :, 128:256] = total[:, 1]


def tree(parts):
    parts = [part.astype(F32) for part in parts]
    while len(parts) > 1:
        parts = [sum(parts[i : i + 2]) for i in range(0, len(parts), 2)]
    return parts[0]


class Swap:
    def __init__(self, shares, scratch):
        self.shares = shares
        self.got, self.part, self.send, self.recv = scratch
        self.face, self.tile = place()
        self.core = lax.rem(self.tile, 2)

    def copy(self, q):
        return remote(
            self.shares.at[pl.ds(4 * q, 4), 1 - self.core],
            self.got.at[pl.ds(4 * q, 4)],
            self.send.at[q],
            self.recv.at[q],
            self.face,
            self.tile + 1 - 2 * self.core,
        )

    def start(self):
        for q in range(4):
            self.copy(q).start()

    def take(self, q, then):
        self.copy(q).wait_recv()

        @pl.loop(4 * q, 4 * q + 4)
        def _(j):
            both = self.shares[j, self.core].astype(F32) + self.got[j].astype(F32)
            self.part[j] = both.astype(BF)
            then(j)

    def finish(self):
        for q in range(4):
            self.copy(q).wait_send()


SWAP_SCRATCH = [
    pltpu.VMEM((NC, SHARE, 128), BF),
    pltpu.VMEM((NC, SHARE, 128), BF),
    DMA((4,)),
    DMA((4,)),
]


class ChipsFirst:
    def __init__(self, part, scratch):
        self.part = part
        self.r1, self.block, self.r2, self.s1, self.q1, self.s2, self.q2 = scratch
        self.face, self.tile = place()
        self.core, self.chip = lax.rem(self.tile, 2), lax.div(self.tile, 2)

    def scatter(self, other, slot):
        return remote(
            self.part.at[other],
            self.r1.at[slot],
            self.s1.at[other],
            self.q1.at[slot],
            self.face,
            2 * other + self.core,
        )

    def send(self, j):
        @pl.when(j != self.chip)
        def _():
            self.scatter(j, self.chip).start()

    def share(self, other, slot):
        return remote(
            self.block, self.r2.at[slot], self.s2.at[other], self.q2.at[slot], other, self.tile
        )

    def middle(self):
        self.r1[self.chip] = self.part[self.chip]

        @pl.loop(1, NC)
        def _(step):
            other = lax.rem(self.chip + step, NC)
            self.scatter(other, other).wait_recv()

        self.block[...] = tree([self.r1[j] for j in range(NC)]).astype(BF)

        @pl.loop(1, NF)
        def _(step):
            self.share(lax.rem(self.face + step, NF), self.face).start()

        self.r2[self.face] = self.block[...]

    def finish(self, out):
        @pl.loop(1, NF)
        def _(step):
            other = lax.rem(self.face + step, NF)
            self.share(other, other).wait_recv()

        put_grads(out, tree([self.r2[j] for j in range(NF)]))

        @pl.loop(1, NC)
        def _(step):
            other = lax.rem(self.chip + step, NC)
            self.scatter(other, other).wait_send()

        @pl.loop(1, NF)
        def _(step):
            other = lax.rem(self.face + step, NF)
            self.share(other, other).wait_send()


CHIPS_SCRATCH = [
    pltpu.VMEM((NC, SHARE, 128), BF),
    pltpu.VMEM((SHARE, 128), BF),
    pltpu.VMEM((NF, SHARE, 128), BF),
    DMA((NC,)),
    DMA((NC,)),
    DMA((NF,)),
    DMA((NF,)),
]


class LineFirst:
    def __init__(self, part, scratch):
        self.part = part
        (
            self.rx,
            self.px,
            self.rz,
            self.block,
            self.rb,
            self.sx,
            self.qx,
            self.sz,
            self.qz,
            self.sb,
            self.qb,
        ) = scratch
        self.face, self.tile = place()
        self.core, self.chip = lax.rem(self.tile, 2), lax.div(self.tile, 2)
        self.x, self.high = lax.div(self.face, 2), lax.rem(self.face, 2)
        self.home = lax.rem(self.chip, 4)
        self.owner = self.home == self.x

    def along(self, other, slot):
        return remote(
            self.part.at[:, other],
            self.rx.at[slot],
            self.sx.at[other],
            self.qx.at[slot],
            2 * other + self.high,
            self.tile,
        )

    def start(self):
        @pl.loop(1, 4)
        def _(step):
            self.along(lax.rem(self.x + step, 4), self.x).start()

    def scatter(self, j, slot):
        return remote(
            self.px.at[j],
            self.rz.at[slot],
            self.sz.at[j],
            self.qz.at[slot],
            self.face,
            2 * (4 * j + self.x) + self.core,
        )

    def middle(self):
        self.rx[self.x] = self.part[:, self.x]

        @pl.loop(1, 4)
        def _(step):
            other = lax.rem(self.x + step, 4)
            self.along(other, other).wait_recv()

        @pl.loop(0, 4)
        def _(j):
            self.px[j] = tree([self.rx[i, j] for i in range(4)]).astype(BF)
            mine = 4 * j + self.x == self.chip

            @pl.when(jnp.logical_not(mine))
            def _():
                self.scatter(j, self.chip).start()

            @pl.when(mine)
            def _():
                self.rz[self.chip] = self.px[j]

    def share(self, other):
        return remote(
            self.block,
            self.rb.at[self.high],
            self.sb.at[other],
            self.qb.at[self.high],
            other,
            self.tile,
        )

    def late(self):
        @pl.when(self.owner)
        def _():
            @pl.loop(1, NC)
            def _(step):
                other = lax.rem(self.chip + step, NC)
                remote(
                    self.px.at[0],
                    self.rz.at[other],
                    self.sz.at[0],
                    self.qz.at[other],
                    self.face,
                    2 * other + self.core,
                ).wait_recv()

            self.block[...] = tree([self.rz[j] for j in range(NC)]).astype(BF)

            @pl.loop(1, NF)
            def _(step):
                self.share(lax.rem(self.face + step, NF)).start()

            self.rb[self.high] = self.block[...]

    def finish(self, out):
        for high in range(2):
            source = 2 * self.home + high

            @pl.when(source != self.face)
            def _():
                remote(
                    self.block,
                    self.rb.at[high],
                    self.sb.at[0],
                    self.qb.at[high],
                    source,
                    self.tile,
                ).wait_recv()

        put_grads(out, tree([self.rb[0], self.rb[1]]))

        @pl.loop(1, 4)
        def _(step):
            other = lax.rem(self.x + step, 4)
            self.along(other, other).wait_send()

        @pl.loop(0, 4)
        def _(j):
            @pl.when(4 * j + self.x != self.chip)
            def _():
                self.scatter(j, self.chip).wait_send()

        @pl.when(self.owner)
        def _():
            @pl.loop(1, NF)
            def _(step):
                self.share(lax.rem(self.face + step, NF)).wait_send()


LINE_SCRATCH = [
    pltpu.VMEM((4, 4, SHARE, 128), BF),
    pltpu.VMEM((4, SHARE, 128), BF),
    pltpu.VMEM((NC, SHARE, 128), BF),
    pltpu.VMEM((SHARE, 128), BF),
    pltpu.VMEM((2, SHARE, 128), BF),
    DMA((4,)),
    DMA((4,)),
    DMA((4,)),
    DMA((NC,)),
    DMA((NF,)),
    DMA((2,)),
]


HALF = RD // 2
N_SUM, N_HALO = len(SUM_SCRATCH), len(HALO_SCRATCH)

WORK_SCRATCH = [
    pltpu.VMEM((HALF, CS, C), BF),
    pltpu.VMEM((3, 3 * C, C), BF),
    pltpu.VMEM((3, 3 * C, C), BF),
    pltpu.VMEM((RD + 2, FS, 3 * C), BF),
    pltpu.VMEM((RD + 2, FS, 3 * C), BF),
    pltpu.VMEM((HALF + 2, CS, 3 * C), BF),
    pltpu.VMEM((HALF + 2, CS, 3 * C), BF),
    pltpu.VMEM((RD, FS, C), BF),
    pltpu.VMEM((HALF, CS, C), BF),
    pltpu.VMEM((RD, FS, C), BF),
    pltpu.VMEM((HALF, CS, C), F32),
    pltpu.VMEM((C, RD * FS), BF),
    pltpu.VMEM((C, HALF * CS), BF),
    pltpu.VMEM((32, C), F32),
    pltpu.VMEM((32, C), F32),
    pltpu.VMEM((NC, 2, SHARE, 128), BF),
    pltpu.VMEM((NC, 2, SHARE, 128), BF),
]


def extended(ref3, field, halo, edge, first, side):
    rows = field.shape[0]

    def put(i, row):
        left, right = edge[pl.ds(first + i, 1), :], edge[pl.ds(first + i + 16, 1), :]
        store_shifted(ref3, i, side(row.astype(F32)), left, right)

    put(0, halo[0])
    put(rows + 1, halo[1])

    @pl.loop(0, rows)
    def _(r):
        put(r + 1, field[r])


def whole_kernel(
    feat, cot, wf_taps, wc_taps, gain, nb, ed,
    output, grad_features, grad_w_fine, grad_w_coarse, grad_gain, *scratch
):
    scratch = list(scratch)

    def take(n):
        got = scratch[:n]
        del scratch[:n]
        return got

    own_a, own_b, buf_a, buf_b, sa, ra, sb, rb = take(N_SUM)
    own_c, own_d, buf_c, buf_d, sc, rc, sd, rd = take(N_SUM)
    halo1_scratch, halo2_scratch = take(N_HALO), take(N_HALO)
    (
        gco, wtf, wtc, x3, u3, c3, v3, fine, coarse_in, grad_fine, gci, gt, gct,
        edge_h, edge_c, shares_f, shares_c,
    ) = take(len(WORK_SCRATCH))
    swap_f = Swap(shares_f, take(len(SWAP_SCRATCH)))
    swap_c = Swap(shares_c, take(len(SWAP_SCRATCH)))
    chips = ChipsFirst(swap_f.part, take(len(CHIPS_SCRATCH)))
    line_scratch = take(len(LINE_SCRATCH))

    halo1 = Halo(feat, gco, halo1_scratch, (nb, ed))
    halo2 = Halo(grad_fine, coarse_in, halo2_scratch, (nb, ed))
    barrier_signal()

    pool, widen = pool_matrix(), spread_matrix()
    own_a[...] = jnp.zeros_like(own_a)
    own_c[...] = jnp.zeros_like(own_c)

    @pl.loop(0, HALF)
    def _(i):
        gco[i] = dot(pool, rows_of(cot, 2 * i, 2)).astype(BF)
        values = rows_of(feat, 2 * i, 2).astype(F32)
        own_a[0:1, :] += jnp.sum(values, axis=0, keepdims=True)
        own_a[1:2, :] += jnp.sum(values * values, axis=0, keepdims=True)

    barrier_wait()
    sum_start(line_a, own_a, buf_a, sa, ra)
    halo1.start()
    back_weights(wc_taps, wtc)
    own_b[...] = sum_finish(line_a, own_a, buf_a, sa, ra)
    sum_start(line_b, own_b, buf_b, sb, rb)
    halo1.middle()
    back_weights(wf_taps, wtf)
    for r in range(HALF):
        gct[:, r * CS : (r + 1) * CS] = gco[r].astype(F32).T.astype(BF)

    first, last, flip_top, flip_bottom = edge_flags(ed)
    halo1.finish((flip_top, flip_bottom))
    edge_c[...] = masked_sides(halo1.sides[...].astype(F32), first, last)

    extended(v3, gco, halo1.hc, edge_c, RD + 2, lambda row: row)
    top, bottom = halo_weights(wtc, flip_top, flip_bottom)
    gci[...] = dot(rows_of(v3, 1, HALF), wtc[1]).reshape(HALF, CS, C)
    gci[1:HALF] += dot(rows_of(v3, 1, HALF - 1), wtc[0]).reshape(HALF - 1, CS, C)
    gci[0 : HALF - 1] += dot(rows_of(v3, 2, HALF - 1), wtc[2]).reshape(HALF - 1, CS, C)
    gci[0] += dot(v3[0], top)
    gci[HALF - 1] += dot(v3[HALF + 1], bottom)

    total = sum_finish(line_b, own_b, buf_b, sb, rb)
    mean, inverse = norm_vectors(total)
    scale = gain[...]

    def hidden(raw):
        act = (raw - mean) * inverse * scale
        return (act * sigmoid(act)).astype(BF).astype(F32)

    edge_h[...] = masked_sides(hidden(halo1.sides[...].astype(F32)), first, last)
    extended(x3, feat, halo1.hf, edge_h, 0, hidden)

    @pl.loop(0, HALF)
    def _(i):
        acc = dot(rows_of(x3, 2 * i, 2), taps_of(wf_taps, 0))
        acc += dot(rows_of(x3, 2 * i + 1, 2), taps_of(wf_taps, 1))
        acc += dot(rows_of(x3, 2 * i + 2, 2), taps_of(wf_taps, 2))
        out = acc.astype(BF)
        fine[pl.ds(2 * i, 2)] = out.reshape(2, FS, C)
        pooled = 0.25 * dot(pool, out)
        gate = sigmoid(pooled)
        coarse_in[i] = (pooled * gate).astype(BF)
        slope = gate * (1.0 + pooled * (1.0 - gate))
        wide = spread(widen, gci[i] * slope * 0.25)
        for r in range(2):
            grad_fine[2 * i + r] = (cot[2 * i + r].astype(F32) + wide).astype(BF)

    halo2.start()

    def fine_gradient(k):
        product = dot(gt[...], rows_of(x3, k, RD))
        for m in range(3):
            put_share(shares_f, 3 * k + m, product[:, m * C : (m + 1) * C])

    for r in range(RD):
        gt[:, r * FS : (r + 1) * FS] = grad_fine[r].astype(F32).T.astype(BF)
    fine_gradient(0)
    halo2.middle()
    fine_gradient(1)
    fine_gradient(2)
    swap_f.start()
    halo2.finish((flip_top, flip_bottom))
    edge_h[...] = masked_sides(halo2.sides[...].astype(F32), first, last)

    extended(c3, coarse_in, halo2.hc, edge_h, RD + 2, lambda row: row)
    for k in range(3):
        product = dot(gct[...], rows_of(c3, k, HALF))
        for m in range(3):
            put_share(shares_c, 3 * k + m, product[:, m * C : (m + 1) * C])
    swap_c.start()
    for q in range(4):
        swap_f.take(q, chips.send)

    extended(u3, grad_fine, halo2.hf, edge_h, 0, lambda row: row)
    top, bottom = halo_weights(wtf, flip_top, flip_bottom)
    ga = grad_features
    ga[1 : RD - 1] = jnp.zeros((RD - 2, FS, C), F32)
    ga[0] = dot(u3[0], top)
    ga[RD - 1] = dot(u3[RD + 1], bottom)
    u3[0] = jnp.zeros((FS, 3 * C), BF)
    u3[RD + 1] = jnp.zeros((FS, 3 * C), BF)

    def back(i):
        grad = dot(rows_of(u3, 2 * i, 2), wtf[0])
        grad += dot(rows_of(u3, 2 * i + 1, 2), wtf[1])
        grad += dot(rows_of(u3, 2 * i + 2, 2), wtf[2])
        grad += rows_of(ga, 2 * i, 2)
        normed = (rows_of(feat, 2 * i, 2).astype(F32) - mean) * inverse
        act = normed * scale
        gate = sigmoid(act)
        grad = grad * (gate * (1.0 + act * (1.0 - gate)))
        ga[pl.ds(2 * i, 2)] = grad.reshape(2, FS, C)
        own_c[0:1, :] += jnp.sum(grad * normed, axis=0, keepdims=True)
        own_c[1:2, :] += jnp.sum(grad, axis=0, keepdims=True)

    pl.loop(0, HALF // 2)(back)
    line = LineFirst(swap_c.part.reshape(4, 4, SHARE, 128), line_scratch)
    for q in range(4):
        swap_c.take(q, lambda j: None)
    line.start()
    pl.loop(HALF // 2, HALF)(back)
    sum_start(line_a, own_c, buf_c, sc, rc)

    @pl.loop(0, HALF)
    def _(i):
        out = dot(c3[i], taps_of(wc_taps, 0)) + dot(c3[i + 1], taps_of(wc_taps, 1)) + dot(c3[i + 2], taps_of(wc_taps, 2))
        wide = spread(widen, out)
        for r in range(2):
            output[2 * i + r] = (fine[2 * i + r].astype(F32) + wide).astype(BF)

    own_d[...] = sum_finish(line_a, own_c, buf_c, sc, rc)
    sum_start(line_b, own_d, buf_d, sd, rd)
    line.middle()
    chips.middle()
    sums = sum_finish(line_b, own_d, buf_d, sd, rd)

    grad_gain[...] = sums[0:1] * (1.0 / CELLS)
    grouped = group_sum(sums * scale) / (CELLS * GROUP)
    group_slope, group_shift = grouped[0:1], grouped[1:2]

    @pl.loop(0, RD)
    def _(r):
        normed = (feat[r].astype(F32) - mean) * inverse
        grad_features[r] = inverse * (scale * ga[r] - group_shift - normed * group_slope)

    line.late()
    chips.finish(grad_w_fine)
    line.finish(grad_w_coarse)
    swap_f.finish()
    swap_c.finish()


def shape(dims, dtype):
    return jax.ShapeDtypeStruct(dims, dtype)


def on_device(features, cotangent, w_fine, w_coarse, gain, neighbors, neighbor_edges):
    outs = [
        shape((RD, FS, C), BF),
        shape((RD, FS, C), F32),
        shape((9, 8, C), F32),
        shape((9, 8, C), F32),
        shape((1, C), F32),
    ]
    output, grad_features, grad_w_fine, grad_w_coarse, grad_gain = pl.pallas_call(
        whole_kernel,
        in_specs=[VM] * 5 + [SM] * 2,
        out_specs=[VM] * len(outs),
        out_shape=outs,
        scratch_shapes=SUM_SCRATCH * 2
        + HALO_SCRATCH * 2
        + WORK_SCRATCH
        + SWAP_SCRATCH * 2
        + CHIPS_SCRATCH
        + LINE_SCRATCH,
        compiler_params=pltpu.CompilerParams(
            vmem_limit_bytes=VMEM_LIMIT, collective_id=1, has_side_effects=True
        ),
    )(
        features[0],
        cotangent[0],
        w_fine,
        w_coarse,
        gain[None],
        neighbors,
        neighbor_edges,
    )
    return (output[None], grad_features[None], grad_w_fine, grad_w_coarse, grad_gain[0])


def solution(mesh):
    return jax.shard_map(
        on_device,
        mesh=mesh,
        in_specs=(
            P("face", "tile", None, None),
            P("face", "tile", None, None),
            P(),
            P(),
            P(),
            P(),
            P(),
        ),
        out_specs=(
            P("face", "tile", None, None),
            P("face", "tile", None, None),
            P(None, "tile", None),
            P(None, "tile", None),
            P(),
        ),
        check_vma=False,
    )
```

time: 144 us -> 97.8 us (0.68)
  the two profiles are of different devices: /device:TPU:248 before, /device:TPU:64 now
where the time goes in v2:
time: 97.8 us; the launch traced here: 97.6 us
  Pallas kernels  88.7 us (91%)
  local copies, waits for them, and re-layouts  8.27 us (8%)
    pallas_call x1, Pallas kernels, on_device(): pl.pallas_call(whole_kernel, in_specs=[VM] * 5 + [SM] * 2, out_specs=[VM]...  88.7 us
    unnamed x15, local copies, waits for them, and re-layouts  8.27 us

profile of v2, /device:TPU:64, one launch (start us, length us, event | category | flops | bytes accessed | tf_op | source)
XLA Modules:
  0.0 97.6 jit_solution(6999413626362751949)
XLA Ops:
  0.6 1.3 %copy.12.nb = s32[8,4]{1,0:T(8,128)} copy(s32[8,4]{0,1:T(4,128)} %param.12) | data formatting | bytes 256 | tf_op args[5]
  2.0 1.3 %copy.13.ed = s32[8,4]{1,0:T(8,128)} copy(s32[8,4]{0,1:T(4,128)} %param.13) | data formatting | bytes 256 | tf_op args[6]
  3.3 88.7 %shard_map.110 = (bf16[8,256,256]{2,1,0:T(8,128)(2,1)}, f32[8,256,256]{2,1,0:T(8,128)}, f32[9,8,256]{2,1,0:T(8,128)}, f32[9,8,256]{2,1,0:T(8,128)}, f32[1,256]{1,0:T(1,128)}) custom-call(bf16[8,256,256]{2,1,0:T(8,128)(2,1)} %bitcast.7, bf16[8,256,256]{2,1,0:T(8,128)(2,1)} %bitcast.8, bf16[9,256,256]{2,1,0:T(8,128)(2,1)} %wf_taps.1, ...), custom_call_target="tpu_custom_call" | custom-call | tf_op jit(solution)/shard_map/pallas_call | solution.py:1024
  92.0 0.0 copy-start
  92.0 2.4 %copy.19 = bf16[1,8,256,256]{3,2,1,0:T(8,128)(2,1)} copy(bf16[1,8,256,256]{3,2,1,0:T(8,128)(2,1)} %bitcast.9) | data formatting | bytes 2097152
  94.4 0.0 copy-done
  94.5 0.0 copy-start.2
  94.5 0.0 copy-start.1
  94.5 0.0 copy-start.3
  94.5 1.3 %copy.20 = f32[1,8,256,256]{3,2,1,0:T(8,128)} copy(f32[1,8,256,256]{3,2,1,0:T(8,128)S(1)} %bitcast.6) | data formatting | bytes 4194304
  95.8 0.0 copy-done.2
  95.8 0.6 copy.21
  96.4 0.0 copy-done.1
  96.4 0.6 copy.22
  97.1 0.0 copy-done.3
  97.1 0.6 copy.23
Async XLA Ops:
  92.0 2.4 %copy-start = (f32[8,256,256]{2,1,0:T(8,128)S(1)}, f32[8,256,256]{2,1,0:T(8,128)}, u32[]{:S(2)}) copy-start(f32[8,256,256]{2,1,0:T(8,128)} %get-tuple-element.11) | copy-start | bytes 6291460
  94.5 1.3 %copy-start.2 = (f32[9,8,256]{2,1,0:T(8,128)S(1)}, f32[9,8,256]{2,1,0:T(8,128)}, u32[]{:S(2)}) copy-start(f32[9,8,256]{2,1,0:T(8,128)} %get-tuple-element.22) | copy-start | bytes 221188
  94.5 2.0 %copy-start.1 = (f32[9,8,256]{2,1,0:T(8,128)S(1)}, f32[9,8,256]{2,1,0:T(8,128)}, u32[]{:S(2)}) copy-start(f32[9,8,256]{2,1,0:T(8,128)} %get-tuple-element.23) | copy-start | bytes 221188
  94.5 2.6 %copy-start.3 = (f32[1,256]{1,0:T(1,128)S(1)}, f32[1,256]{1,0:T(1,128)}, u32[]{:S(2)}) copy-start(f32[1,256]{1,0:T(1,128)} %get-tuple-element.14) | copy-start | bytes 3076

commit v3 on v2

v3 whole, which is shorter than its diff:
```python
import jax
import jax.numpy as jnp
from jax import lax
from jax.experimental import pallas as pl
from jax.experimental.pallas import tpu as pltpu
from jax.sharding import PartitionSpec as P

BF = jnp.bfloat16
F32 = jnp.float32
MESH = pl.DeviceIdType.MESH
NF = 8
NT = 32
NZ = 16
RD = 8
FS = 256
CS = 128
C = 256
GROUP = 8
SLOTS = 16
CELLS = NF * FS * FS
VMEM_LIMIT = 60 * 1024 * 1024

VM = pl.BlockSpec(memory_space=pltpu.VMEM)
SM = pl.BlockSpec(memory_space=pltpu.SMEM)
DMA = pltpu.SemaphoreType.DMA


def remote(src, dst, send, recv, face, tile):
    return pltpu.make_async_remote_copy(
        src_ref=src,
        dst_ref=dst,
        send_sem=send,
        recv_sem=recv,
        device_id=(face, tile),
        device_id_type=MESH,
    )


def place():
    return lax.axis_index("face"), lax.axis_index("tile")


def is_rim(tile):
    return (tile == 0) | (tile == NT - 1)


def slot_device(slot):
    return lax.div(slot, 2), (NT - 1) * lax.rem(slot, 2)


def my_slot(face, tile):
    return 2 * face + jnp.where(tile == NT - 1, 1, 0)


def multiple(value, of):
    return pl.multiple_of(value * of, of)


def signal(barrier, face, tile):
    pl.semaphore_signal(barrier, inc=1, device_id=(face, tile), device_id_type=MESH)


def line_a(face, tile, step):
    mine = lax.rem(tile, NZ)
    other = lax.rem(mine + step, NZ)
    return mine, other, (face, tile - mine + other)


def line_b(face, tile, step):
    mine = face * 2 + lax.div(tile, NZ)
    other = lax.rem(mine + step, 2 * NF)
    return mine, other, (lax.div(other, 2), lax.rem(other, 2) * NZ + lax.rem(tile, NZ))


def barrier_signal():
    face, tile = place()
    barrier = pltpu.get_barrier_semaphore()
    across = lax.rem(tile + NZ, NT)
    across = across - lax.rem(across, NZ) + lax.rem(tile, 2)

    @pl.loop(1, NZ)
    def _(step):
        for line in (line_a, line_b):
            _, _, device = line(face, tile, step)
            signal(barrier, *device)

    @pl.loop(0, NZ // 2)
    def _(z):
        signal(barrier, face, across + 2 * z)

    signal(barrier, face, lax.rem(tile + 1, NT))
    signal(barrier, face, lax.rem(tile + NT - 1, NT))

    @pl.when(is_rim(tile))
    def _():
        mine = my_slot(face, tile)

        @pl.loop(1, SLOTS)
        def _(step):
            signal(barrier, *slot_device(lax.rem(mine + step, SLOTS)))


def barrier_wait():
    _, tile = place()
    barrier = pltpu.get_barrier_semaphore()
    count = 2 * (NZ - 1) + NZ // 2 + 2

    @pl.when(is_rim(tile))
    def _():
        pl.semaphore_wait(barrier, count + SLOTS - 1)

    @pl.when(~is_rim(tile))
    def _():
        pl.semaphore_wait(barrier, count)


def sum_start(line, own, buf, send, recv):
    face, tile = place()

    @pl.loop(1, NZ)
    def _(step):
        mine, _, device = line(face, tile, step)
        remote(own, buf.at[mine], send, recv, *device).start()

    mine, _, _ = line(face, tile, 0)
    buf[mine] = own[...]


def sum_finish(line, own, buf, send, recv):
    face, tile = place()
    _, _, device = line(face, tile, 1)
    arrived = buf.at[pl.ds(0, NZ - 1)]
    copies = remote(arrived, arrived, send, recv, *device)
    copies.wait_recv()
    total = buf[0]
    for i in range(1, NZ):
        total = total + buf[i]
    copies.wait_send()
    return total


SUM_SCRATCH = [
    pltpu.VMEM((2, C), F32),
    pltpu.VMEM((2, C), F32),
    pltpu.VMEM((NZ, 2, C), F32),
    pltpu.VMEM((NZ, 2, C), F32),
    DMA,
    DMA,
    DMA,
    DMA,
]

RIM = C + 128

HALO_SCRATCH = [
    pltpu.VMEM((2, FS, C), BF),
    pltpu.VMEM((2, CS, C), BF),
    pltpu.VMEM((SLOTS, 16, RIM), BF),
    pltpu.VMEM((SLOTS, 16, RIM), BF),
    pltpu.VMEM((SLOTS, 16, RIM), BF),
    pltpu.VMEM((SLOTS, 16, RIM), BF),
    pltpu.VMEM((32, C), F32),
    pltpu.VMEM((32, C), BF),
    pltpu.VMEM((NF, 32, C), BF),
    pltpu.VMEM((32, C), BF),
] + [DMA] * 10


class Halo:
    def __init__(self, fine, coarse, scratch, tables):
        self.fine, self.coarse = fine, coarse
        (
            self.hf,
            self.hc,
            self.rim,
            self.r1,
            self.st,
            self.r2,
            self.rows,
            self.srec,
            self.sall,
            self.sides,
            self.fs,
            self.fr,
            self.cs,
            self.cr,
            self.s1,
            self.q1,
            self.s2,
            self.q2,
            self.ss,
            self.sr,
        ) = scratch
        self.nb, self.ed = tables
        self.face, self.tile = place()
        self.slot = my_slot(self.face, self.tile)

    def rows_start(self):
        up = lax.rem(self.tile + 1, NT)
        down = lax.rem(self.tile + NT - 1, NT)
        for field, halo, send, recv in (
            (self.fine, self.hf, self.fs, self.fr),
            (self.coarse, self.hc, self.cs, self.cr),
        ):
            last = field.shape[0] - 1
            remote(field.at[last], halo.at[0], send, recv, self.face, up).start()
            remote(field.at[0], halo.at[1], send, recv, self.face, down).start()

    def rows_wait(self):
        up = lax.rem(self.tile + 1, NT)
        for halo, send, recv in ((self.hf, self.fs, self.fr), (self.hc, self.cs, self.cr)):
            both = remote(halo, halo, send, recv, self.face, up)
            both.wait_recv()
            both.wait_send()

    def rim_partner(self, step):
        other = lax.rem(self.slot + step, SLOTS)
        return other, slot_device(other)

    def rim_wait(self, buf, send, recv):
        _, device = self.rim_partner(1)
        arrived = buf.at[pl.ds(0, SLOTS - 1)]
        copies = remote(arrived, arrived, send, recv, *device)
        copies.wait_recv()
        copies.wait_send()

    def start(self):
        @pl.when(is_rim(self.tile))
        def _():
            fine_row = jnp.where(self.tile == 0, 0, RD - 1)
            coarse_row = jnp.where(self.tile == 0, 0, RD // 2 - 1)
            self.rim[:, :, 0:C] = self.fine[fine_row].reshape(SLOTS, 16, C)
            cells = self.coarse[coarse_row]
            self.rim[0:8, :, C:RIM] = cells[:, 0:128].reshape(8, 16, 128)
            self.rim[8:16, :, C:RIM] = cells[:, 128:256].reshape(8, 16, 128)

            @pl.loop(1, SLOTS)
            def _(step):
                other, device = self.rim_partner(step)
                remote(self.rim.at[other], self.r1.at[self.slot], self.s1, self.q1, *device).start()

            self.r1[self.slot] = self.rim[self.slot]

        self.rows_start()

    def middle(self):
        @pl.when(is_rim(self.tile))
        def _():
            self.rim_wait(self.r1, self.s1, self.q1)

            @pl.loop(0, SLOTS)
            def _(slot):
                face, edge = lax.div(slot, 2), 2 * lax.rem(slot, 2)
                source = 2 * self.nb[face, edge] + lax.div(self.ed[face, edge], 2)
                self.st[slot] = self.r1[source]

            @pl.loop(1, SLOTS)
            def _(step):
                other, device = self.rim_partner(step)
                remote(self.st.at[other], self.r2.at[self.slot], self.s2, self.q2, *device).start()

            self.r2[self.slot] = self.st[self.slot]

        self.rows_wait()
        fine_rows = [self.hf.at[0]] + [self.fine.at[r] for r in range(RD)] + [self.hf.at[1]]
        coarse_rows = [self.hc.at[0]] + [self.coarse.at[r] for r in range(RD // 2)]
        coarse_rows += [self.hc.at[1]]
        for i, row in enumerate(fine_rows + coarse_rows):
            side = row.shape[0]
            self.rows[i : i + 1, :] = row[0:16, :].astype(F32)[0:1]
            self.rows[16 + i : 17 + i, :] = row[side - 16 : side, :].astype(F32)[15:16]
        self.srec[...] = self.rows[...].astype(BF)

        @pl.loop(1, NF)
        def _(step):
            other = lax.rem(self.face + step, NF)
            remote(
                self.srec, self.sall.at[self.face], self.ss, self.sr, other, self.tile
            ).start()

        self.sall[self.face] = self.srec[...]

    def finish(self, flips):
        @pl.when(is_rim(self.tile))
        def _():
            self.rim_wait(self.r2, self.s2, self.q2)
            flip_top, flip_bottom = flips
            flip = jnp.where(self.tile == 0, flip_top, flip_bottom)
            edge = jnp.where(self.tile == 0, 0, 1)
            fine = self.r2[:, :, 0:C].reshape(FS, C)
            coarse = jnp.concatenate(
                [
                    self.r2[0:8, :, C:RIM].reshape(CS, 128),
                    self.r2[8:16, :, C:RIM].reshape(CS, 128),
                ],
                axis=1,
            )
            self.hf[edge] = dot(rim_matrix(FS, flip), fine).astype(BF)
            self.hc[edge] = dot(rim_matrix(CS, flip), coarse).astype(BF)

        other = lax.rem(self.face + 1, NF)
        arrived = self.sall.at[pl.ds(0, NF - 1)]
        copies = remote(arrived, arrived, self.ss, self.sr, other, self.tile)
        copies.wait_recv()
        copies.wait_send()
        left_face, right_face = self.nb[self.face, 3], self.nb[self.face, 1]
        self.sides[0:16, :] = self.sall[left_face, 16:32, :]
        self.sides[16:32, :] = self.sall[right_face, 0:16, :]


def iota(shape, dim):
    return lax.broadcasted_iota(jnp.int32, shape, dim)


def dot(a, b):
    return jnp.dot(a, b, preferred_element_type=F32)


def sigmoid(values):
    return 0.5 * jnp.tanh(0.5 * values) + 0.5


def pool_matrix():
    row, col = iota((CS, 2 * FS), 0), iota((CS, 2 * FS), 1)
    return jnp.where(lax.div(lax.rem(col, FS), 2) == row, 1.0, 0.0).astype(BF)


def spread_matrix():
    row, col = iota((FS, 2 * CS), 0), iota((FS, 2 * CS), 1)
    return jnp.where(lax.rem(col, CS) == lax.div(row, 2), 1.0, 0.0).astype(BF)


def spread(matrix, values):
    high = values.astype(BF)
    low = (values - high.astype(F32)).astype(BF)
    return dot(matrix, jnp.concatenate([high, low], axis=0))


def rim_matrix(side, flip):
    row, col = iota((side, side), 0), iota((side, side), 1)
    source = jnp.where(flip, side - 1 - row, row)
    return jnp.where(col == source, 1.0, 0.0).astype(BF)


def store_shifted(ref, row, values, left, right):
    n = values.shape[0]
    position = iota(values.shape, 0)
    before = jnp.where(position == 0, left, pltpu.roll(values, 1, 0))
    after = jnp.where(position == n - 1, right, pltpu.roll(values, n - 1, 0))
    ref[row, :, 0:C] = before.astype(BF)
    ref[row, :, C : 2 * C] = values.astype(BF)
    ref[row, :, 2 * C : 3 * C] = after.astype(BF)


def group_sum(values):
    lane = iota(values.shape, 1)
    for width in (1, 2, 4):
        up = pltpu.roll(values, width, 1)
        down = pltpu.roll(values, C - width, 1)
        values = values + jnp.where(lax.rem(lax.div(lane, width), 2) == 0, down, up)
    return values


def norm_vectors(total):
    grouped = group_sum(total) / (CELLS * GROUP)
    mean, second = grouped[0:1], grouped[1:2]
    return mean, lax.rsqrt(second - mean * mean + 1e-05)


def edge_flags(ed_ref):
    face, tile = place()
    first, last = tile == 0, tile == NT - 1
    flip_top = first & (ed_ref[face, 0] != 2)
    flip_bottom = last & (ed_ref[face, 2] != 0)
    return first, last, flip_top, flip_bottom


def masked_sides(sides, first, last):
    row = lax.rem(iota(sides.shape, 0), 16)
    top = (row == 0) | (row == RD + 2)
    bottom = (row == RD + 1) | (row == 15)
    zero = (top & first) | (bottom & last)
    return jnp.where(zero, 0.0, sides)


def back_weights(w_ref, out_ref):
    for k in range(3):
        for m in range(3):
            tap = w_ref[8 - (3 * k + m)].astype(F32)
            out_ref[k, m * C : (m + 1) * C, :] = tap.T.astype(BF)


def halo_weights(wt_ref, flip_top, flip_bottom):
    def turned(k):
        return jnp.concatenate(
            [wt_ref[k, (2 - m) * C : (3 - m) * C, :] for m in range(3)], axis=0
        )

    top = jnp.where(flip_top, turned(2), wt_ref[0])
    bottom = jnp.where(flip_bottom, turned(0), wt_ref[2])
    return top, bottom


def rows_of(ref, start, count):
    _, side, width = ref.shape
    return ref[pl.ds(start, count)].reshape(count * side, width)


def taps_of(ref, k):
    return ref[3 * k : 3 * k + 3].reshape(3 * C, C)


SHARE = 144
NC = 16


def put_share(shares, tap, product):
    turned = product.T.reshape(4, 4, 2, 8, C)
    halves = [turned[..., :128], turned[..., 128:]]
    shares[:, :, :, 16 * tap : 16 * tap + 16, :] = jnp.concatenate(halves, axis=3).astype(BF)


def put_grads(out, total):
    total = (total * (1.0 / CELLS)).reshape(9, 2, 8, 128)
    out[:, :, 0:128] = total[:, 0]
    out[:, :, 128:256] = total[:, 1]


def tree(parts):
    parts = [part.astype(F32) for part in parts]
    while len(parts) > 1:
        parts = [sum(parts[i : i + 2]) for i in range(0, len(parts), 2)]
    return parts[0]


CUT = 80
LANES = ((0, CUT), (CUT, SHARE - CUT))

REDUCE_SCRATCH = [
    pltpu.VMEM((4, 4, 2, SHARE, 128), BF),
    pltpu.VMEM((4, 4, SHARE, 128), BF),
    pltpu.VMEM((4, 4, SHARE, 128), BF),
    pltpu.VMEM((2, 4, CUT, 128), BF),
    pltpu.VMEM((2, 4, SHARE - CUT, 128), BF),
    pltpu.VMEM((4, CUT, 128), BF),
    pltpu.VMEM((4, SHARE - CUT, 128), BF),
    pltpu.VMEM((4, CUT, 128), BF),
    pltpu.VMEM((4, SHARE - CUT, 128), BF),
    pltpu.VMEM((4, SHARE, 128), BF),
    pltpu.VMEM((NC, SHARE, 128), BF),
    pltpu.VMEM((SHARE, 128), BF),
    pltpu.VMEM((2, SHARE, 128), BF),
    DMA((3,)),
    DMA((3,)),
    DMA((2,)),
    DMA((2,)),
    DMA((2,)),
    DMA((2,)),
    DMA((4,)),
    DMA,
    DMA,
    DMA((2,)),
]


class Reduce:
    def __init__(self, scratch):
        (
            self.shares,
            self.got,
            self.part,
            r0,
            r1,
            t0,
            t1,
            u0,
            u1,
            self.px,
            self.rz,
            self.block,
            self.rb,
            self.s0,
            self.q0,
            self.sa,
            self.qa,
            self.sc,
            self.qc,
            self.sz,
            self.qz,
            self.sb,
            self.qb,
        ) = scratch
        self.one, self.on, self.two = (r0, r1), (t0, t1), (u0, u1)
        self.face, self.tile = place()
        self.core, self.chip = lax.rem(self.tile, 2), lax.div(self.tile, 2)
        self.x, self.high = lax.div(self.face, 2), lax.rem(self.face, 2)
        self.home = lax.rem(self.chip, 4)
        self.owner = self.home == self.x
        near = self.x + 1 - 2 * lax.rem(self.x, 2)
        self.partner = (near, 3 - self.x)

    def swap(self, k):
        rows = pl.ds(48 * k, 48)
        return remote(
            self.shares.at[:, :, 1 - self.core, rows, :],
            self.got.at[:, :, rows, :],
            self.s0.at[k],
            self.q0.at[k],
            self.face,
            self.tile + 1 - 2 * self.core,
        )

    def swap_start(self, k):
        self.swap(k).start()

    def across(self, way, src, dst, send, recv):
        return remote(src, dst, send, recv, 2 * self.partner[way] + self.high, self.tile)

    def first(self, way, i):
        other = self.partner[way]
        beyond = 3 - other if way == 0 else other + 1 - 2 * lax.rem(other, 2)
        start, rows = LANES[way]
        return self.across(
            way,
            self.part.at[:, (other, beyond)[i], pl.ds(start, rows), :],
            self.one[way].at[i],
            self.sa.at[way],
            self.qa.at[way],
        )

    def first_wait(self, way):
        return self.across(way, self.one[way], self.one[way], self.sa.at[way], self.qa.at[way])

    def second(self, way):
        return self.across(1 - way, self.on[way], self.two[way], self.sc.at[way], self.qc.at[way])

    def swap_take(self):
        for k in range(3):
            self.swap(k).wait_recv()

        @pl.loop(0, 4)
        def _(j):
            for h in range(4):
                both = self.shares[j, h, self.core].astype(F32) + self.got[j, h].astype(F32)
                self.part[j, h] = both.astype(BF)

        for way in range(2):
            for i in range(2):
                self.first(way, i).start()

    def first_take(self):
        for way in range(2):
            self.first_wait(way).wait_recv()
            start, rows = LANES[way]
            span = pl.ds(start, rows)
            mine = self.part[:, self.partner[1 - way], span, :].astype(F32)
            self.on[way][...] = (mine + self.one[way][1].astype(F32)).astype(BF)
            self.second(way).start()

    def second_take(self):
        for way in range(2):
            self.second(way).wait_recv()
            start, rows = LANES[way]
            mine = self.part[:, self.x, pl.ds(start, rows), :].astype(F32)
            total = mine + self.one[way][0].astype(F32) + self.two[way][...].astype(F32)
            self.px[:, start : start + rows, :] = total.astype(BF)

        @pl.loop(0, 4)
        def _(j):
            mine = 4 * j + self.x == self.chip

            @pl.when(jnp.logical_not(mine))
            def _():
                self.scatter(j).start()

            @pl.when(mine)
            def _():
                self.rz[self.chip] = self.px[j]

    def scatter(self, j):
        return remote(
            self.px.at[j],
            self.rz.at[self.chip],
            self.sz.at[j],
            self.qz,
            self.face,
            2 * (4 * j + self.x) + self.core,
        )

    def share(self, other):
        return remote(
            self.block, self.rb.at[self.high], self.sb, self.qb.at[self.high], other, self.tile
        )

    def chips_take(self):
        @pl.when(self.owner)
        def _():
            arrived = self.rz.at[pl.ds(0, NC - 1)]
            other = lax.rem(self.chip + 1, NC)
            remote(
                arrived, arrived, self.sb, self.qz, self.face, 2 * other + self.core
            ).wait_recv()
            self.block[...] = tree([self.rz[j] for j in range(NC)]).astype(BF)

            @pl.loop(1, NF)
            def _(step):
                self.share(lax.rem(self.face + step, NF)).start()

            self.rb[self.high] = self.block[...]

    def finish(self, out):
        for high in range(2):
            source = 2 * self.home + high

            @pl.when(source != self.face)
            def _():
                remote(
                    self.block, self.rb.at[high], self.sb, self.qb.at[high], source, self.tile
                ).wait_recv()

        put_grads(out, tree([self.rb[0], self.rb[1]]))

        for k in range(3):
            self.swap(k).wait_send()
        for way in range(2):
            self.first_wait(way).wait_send()
            self.second(way).wait_send()

        @pl.loop(0, 4)
        def _(j):
            @pl.when(4 * j + self.x != self.chip)
            def _():
                self.scatter(j).wait_send()

        @pl.when(self.owner)
        def _():
            sent = self.rz.at[pl.ds(0, NF - 1)]
            remote(
                sent, sent, self.sb, self.qz, lax.rem(self.face + 1, NF), self.tile
            ).wait_send()


HALF = RD // 2
N_SUM, N_HALO = len(SUM_SCRATCH), len(HALO_SCRATCH)

ANY = pl.BlockSpec(memory_space=pl.ANY)

WORK_SCRATCH = [
    pltpu.SMEM((NF, 4), jnp.int32),
    pltpu.SMEM((NF, 4), jnp.int32),
    pltpu.VMEM((9, C, C), BF),
    pltpu.VMEM((9, C, C), BF),
    pltpu.VMEM((HALF, CS, C), BF),
    pltpu.VMEM((3, 3 * C, C), BF),
    pltpu.VMEM((3, 3 * C, C), BF),
    pltpu.VMEM((RD + 2, FS, 3 * C), BF),
    pltpu.VMEM((RD + 2, FS, 3 * C), BF),
    pltpu.VMEM((HALF + 2, CS, 3 * C), BF),
    pltpu.VMEM((HALF + 2, CS, 3 * C), BF),
    pltpu.VMEM((RD, FS, C), BF),
    pltpu.VMEM((HALF, CS, C), BF),
    pltpu.VMEM((RD, FS, C), BF),
    pltpu.VMEM((RD, FS, C), F32),
    pltpu.VMEM((HALF, CS, C), F32),
    pltpu.VMEM((C, RD * FS), BF),
    pltpu.VMEM((C, HALF * CS), BF),
    pltpu.VMEM((32, C), F32),
    pltpu.VMEM((32, C), F32),
    DMA((6,)),
]


def extended(ref3, field, halo, edge, first, side):
    rows = field.shape[0]

    def put(i, row):
        left, right = edge[pl.ds(first + i, 1), :], edge[pl.ds(first + i + 16, 1), :]
        store_shifted(ref3, i, side(row.astype(F32)), left, right)

    put(0, halo[0])
    put(rows + 1, halo[1])

    @pl.loop(0, rows)
    def _(r):
        put(r + 1, field[r])


def whole_kernel(
    feat, cot, wf_any, wc_any, gain, nb_any, ed_any,
    output, grad_act, grad_w_fine, grad_w_coarse, grad_gain, vectors, *scratch
):
    scratch = list(scratch)

    def take(n):
        got = scratch[:n]
        del scratch[:n]
        return got

    own_a, own_b, buf_a, buf_b, sa, ra, sb, rb = take(N_SUM)
    own_c, own_d, buf_c, buf_d, sc, rc, sd, rd = take(N_SUM)
    halo1_scratch, halo2_scratch = take(N_HALO), take(N_HALO)
    (
        nb, ed, wf_taps, wc_taps, gco, wtf, wtc, x3, u3, c3, v3, fine, coarse_in, grad_fine,
        ga, gci, gt, gct, edge_h, edge_c, local,
    ) = take(len(WORK_SCRATCH))
    reduce_f = Reduce(take(len(REDUCE_SCRATCH)))
    reduce_c = Reduce(take(len(REDUCE_SCRATCH)))

    barrier_signal()
    loads = [
        pltpu.make_async_copy(src, dst, local.at[i])
        for i, (src, dst) in enumerate(
            ((nb_any, nb), (ed_any, ed), (wf_any, wf_taps), (wc_any, wc_taps))
        )
    ]
    for load in loads:
        load.start()
    halo1 = Halo(feat, gco, halo1_scratch, (nb, ed))
    halo2 = Halo(grad_fine, coarse_in, halo2_scratch, (nb, ed))

    pool, widen = pool_matrix(), spread_matrix()
    own_a[...] = jnp.zeros_like(own_a)
    own_c[...] = jnp.zeros_like(own_c)

    @pl.loop(0, HALF)
    def _(i):
        gco[i] = dot(pool, rows_of(cot, 2 * i, 2)).astype(BF)
        values = rows_of(feat, 2 * i, 2).astype(F32)
        own_a[0:1, :] += jnp.sum(values, axis=0, keepdims=True)
        own_a[1:2, :] += jnp.sum(values * values, axis=0, keepdims=True)

    barrier_wait()
    sum_start(line_a, own_a, buf_a, sa, ra)
    halo1.start()
    for load in loads:
        load.wait()
    back_weights(wc_taps, wtc)
    own_b[...] = sum_finish(line_a, own_a, buf_a, sa, ra)
    sum_start(line_b, own_b, buf_b, sb, rb)
    halo1.middle()
    back_weights(wf_taps, wtf)
    for r in range(HALF):
        gct[:, r * CS : (r + 1) * CS] = gco[r].astype(F32).T.astype(BF)

    first, last, flip_top, flip_bottom = edge_flags(ed)
    halo1.finish((flip_top, flip_bottom))
    edge_c[...] = masked_sides(halo1.sides[...].astype(F32), first, last)

    extended(v3, gco, halo1.hc, edge_c, RD + 2, lambda row: row)
    top, bottom = halo_weights(wtc, flip_top, flip_bottom)
    gci[...] = dot(rows_of(v3, 1, HALF), wtc[1]).reshape(HALF, CS, C)
    gci[1:HALF] += dot(rows_of(v3, 1, HALF - 1), wtc[0]).reshape(HALF - 1, CS, C)
    gci[0 : HALF - 1] += dot(rows_of(v3, 2, HALF - 1), wtc[2]).reshape(HALF - 1, CS, C)
    gci[0] += dot(v3[0], top)
    gci[HALF - 1] += dot(v3[HALF + 1], bottom)

    total = sum_finish(line_b, own_b, buf_b, sb, rb)
    mean, inverse = norm_vectors(total)
    scale = gain[...]

    def hidden(raw):
        act = (raw - mean) * inverse * scale
        return (act * sigmoid(act)).astype(BF).astype(F32)

    edge_h[...] = masked_sides(hidden(halo1.sides[...].astype(F32)), first, last)
    extended(x3, feat, halo1.hf, edge_h, 0, hidden)

    def forward(i):
        acc = dot(rows_of(x3, 2 * i, 2), taps_of(wf_taps, 0))
        acc += dot(rows_of(x3, 2 * i + 1, 2), taps_of(wf_taps, 1))
        acc += dot(rows_of(x3, 2 * i + 2, 2), taps_of(wf_taps, 2))
        out = acc.astype(BF)
        fine[pl.ds(2 * i, 2)] = out.reshape(2, FS, C)
        pooled = 0.25 * dot(pool, out)
        gate = sigmoid(pooled)
        coarse_in[i] = (pooled * gate).astype(BF)
        slope = gate * (1.0 + pooled * (1.0 - gate))
        wide = spread(widen, gci[i] * slope * 0.25)
        for r in range(2):
            grad_fine[2 * i + r] = (cot[2 * i + r].astype(F32) + wide).astype(BF)

    @pl.loop(0, 2)
    def _(i):
        forward((HALF - 1) * i)

    halo2.start()
    pl.loop(1, HALF - 1)(forward)

    def fine_gradient(k):
        product = dot(gt[...], rows_of(x3, k, RD))
        for m in range(3):
            put_share(reduce_f.shares, 3 * k + m, product[:, m * C : (m + 1) * C])
        reduce_f.swap_start(k)

    for r in range(RD):
        gt[:, r * FS : (r + 1) * FS] = grad_fine[r].astype(F32).T.astype(BF)
    halo2.middle()
    for k in range(3):
        fine_gradient(k)
    halo2.finish((flip_top, flip_bottom))
    edge_h[...] = masked_sides(halo2.sides[...].astype(F32), first, last)
    reduce_f.swap_take()

    extended(c3, coarse_in, halo2.hc, edge_h, RD + 2, lambda row: row)
    for k in range(3):
        product = dot(gct[...], rows_of(c3, k, HALF))
        for m in range(3):
            put_share(reduce_c.shares, 3 * k + m, product[:, m * C : (m + 1) * C])
        reduce_c.swap_start(k)
    reduce_f.first_take()

    extended(u3, grad_fine, halo2.hf, edge_h, 0, lambda row: row)
    top, bottom = halo_weights(wtf, flip_top, flip_bottom)
    reduce_c.swap_take()
    ga[1 : RD - 1] = jnp.zeros((RD - 2, FS, C), F32)
    ga[0] = dot(u3[0], top)
    ga[RD - 1] = dot(u3[RD + 1], bottom)
    u3[0] = jnp.zeros((FS, 3 * C), BF)
    u3[RD + 1] = jnp.zeros((FS, 3 * C), BF)

    def back(i):
        grad = dot(rows_of(u3, 2 * i, 2), wtf[0])
        grad += dot(rows_of(u3, 2 * i + 1, 2), wtf[1])
        grad += dot(rows_of(u3, 2 * i + 2, 2), wtf[2])
        grad += rows_of(ga, 2 * i, 2)
        normed = (rows_of(feat, 2 * i, 2).astype(F32) - mean) * inverse
        act = normed * scale
        gate = sigmoid(act)
        grad = grad * (gate * (1.0 + act * (1.0 - gate)))
        ga[pl.ds(2 * i, 2)] = grad.reshape(2, FS, C)
        own_c[0:1, :] += jnp.sum(grad * normed, axis=0, keepdims=True)
        own_c[1:2, :] += jnp.sum(grad, axis=0, keepdims=True)

    pl.loop(0, HALF // 2)(back)
    reduce_f.second_take()
    reduce_c.first_take()
    pl.loop(HALF // 2, HALF)(back)
    sum_start(line_a, own_c, buf_c, sc, rc)
    store_act = pltpu.make_async_copy(ga, grad_act, local.at[4])
    store_act.start()
    reduce_c.second_take()

    @pl.loop(0, HALF)
    def _(i):
        out = dot(c3[i], taps_of(wc_taps, 0))
        out += dot(c3[i + 1], taps_of(wc_taps, 1))
        out += dot(c3[i + 2], taps_of(wc_taps, 2))
        wide = spread(widen, out)
        for r in range(2):
            fine[2 * i + r] = (fine[2 * i + r].astype(F32) + wide).astype(BF)

    store_output = pltpu.make_async_copy(fine, output, local.at[5])
    store_output.start()
    own_d[...] = sum_finish(line_a, own_c, buf_c, sc, rc)
    sum_start(line_b, own_d, buf_d, sd, rd)
    reduce_f.chips_take()
    reduce_c.chips_take()
    sums = sum_finish(line_b, own_d, buf_d, sd, rd)

    grad_gain[...] = sums[0:1] * (1.0 / CELLS)
    grouped = group_sum(sums * scale) / (CELLS * GROUP)
    group_slope, group_shift = grouped[0:1], grouped[1:2]
    for i, vector in enumerate((mean, inverse, scale, group_shift, group_slope)):
        vectors[i : i + 1, :] = vector
    reduce_f.finish(grad_w_fine)
    reduce_c.finish(grad_w_coarse)
    store_act.wait()
    store_output.wait()


def last_kernel(
    feat, ga, vectors, output_in, wf_in, wc_in, gain_in,
    output, grad_features, wf_out, wc_out, gain_out, feat_v, ga_v, out_v, sems
):
    passed = [
        pltpu.make_async_copy(src, dst, sems.at[i])
        for i, (src, dst) in enumerate(
            ((output_in, output), (wf_in, wf_out), (wc_in, wc_out), (gain_in, gain_out))
        )
    ]

    def rows(q):
        return pl.ds(2 * q, 2)

    loads = [
        (
            pltpu.make_async_copy(feat.at[rows(q)], feat_v.at[rows(q)], sems.at[4 + 3 * q]),
            pltpu.make_async_copy(ga.at[rows(q)], ga_v.at[rows(q)], sems.at[5 + 3 * q]),
        )
        for q in range(HALF)
    ]
    stores = [
        pltpu.make_async_copy(out_v.at[rows(q)], grad_features.at[rows(q)], sems.at[6 + 3 * q])
        for q in range(HALF)
    ]
    for load in loads:
        for copy in load:
            copy.start()
    for copy in passed:
        copy.start()
    mean, inverse, scale = vectors[0:1], vectors[1:2], vectors[2:3]
    group_shift, group_slope = vectors[3:4], vectors[4:5]
    for q in range(HALF):
        for copy in loads[q]:
            copy.wait()
        for r in (2 * q, 2 * q + 1):
            normed = (feat_v[r].astype(F32) - mean) * inverse
            out_v[r] = inverse * (scale * ga_v[r] - group_shift - normed * group_slope)
        stores[q].start()
    for copy in stores + passed:
        copy.wait()


def shape(dims, dtype):
    return jax.ShapeDtypeStruct(dims, dtype)


def on_device(features, cotangent, w_fine, w_coarse, gain, neighbors, neighbor_edges):
    outs = [
        shape((RD, FS, C), BF),
        shape((RD, FS, C), F32),
        shape((9, 8, C), F32),
        shape((9, 8, C), F32),
        shape((1, C), F32),
    ]
    output, grad_act, grad_w_fine, grad_w_coarse, grad_gain, vectors = pl.pallas_call(
        whole_kernel,
        in_specs=[VM, VM, ANY, ANY, VM, ANY, ANY],
        out_specs=[ANY, ANY, VM, VM, VM, VM],
        out_shape=outs + [shape((8, C), F32)],
        scratch_shapes=SUM_SCRATCH * 2
        + HALO_SCRATCH * 2
        + WORK_SCRATCH
        + REDUCE_SCRATCH * 2,
        compiler_params=pltpu.CompilerParams(
            vmem_limit_bytes=VMEM_LIMIT, collective_id=1, has_side_effects=True
        ),
    )(features[0], cotangent[0], w_fine, w_coarse, gain[None], neighbors, neighbor_edges)
    output, grad_features, grad_w_fine, grad_w_coarse, grad_gain = pl.pallas_call(
        last_kernel,
        in_specs=[ANY, ANY, VM] + [ANY] * 4,
        out_specs=[ANY] * 5,
        out_shape=outs,
        scratch_shapes=[
            pltpu.VMEM((RD, FS, C), BF),
            pltpu.VMEM((RD, FS, C), F32),
            pltpu.VMEM((RD, FS, C), F32),
            DMA((4 + 3 * HALF,)),
        ],
        compiler_params=pltpu.CompilerParams(vmem_limit_bytes=VMEM_LIMIT),
    )(features[0], grad_act, vectors, output, grad_w_fine, grad_w_coarse, grad_gain)
    return (output[None], grad_features[None], grad_w_fine, grad_w_coarse, grad_gain[0])


def solution(mesh):
    return jax.shard_map(
        on_device,
        mesh=mesh,
        in_specs=(
            P("face", "tile", None, None),
            P("face", "tile", None, None),
            P(),
            P(),
            P(),
            P(),
            P(),
        ),
        out_specs=(
            P("face", "tile", None, None),
            P("face", "tile", None, None),
            P(None, "tile", None),
            P(None, "tile", None),
            P(),
        ),
        check_vma=False,
    )
```

time: 97.8 us -> 113 us (1.16)
  the two profiles are of different devices: /device:TPU:64 before, /device:TPU:4 now
where the time goes in v3:
time: 113 us
  Pallas kernels  110 us (97%)
  local copies, waits for them, and re-layouts  2.7 us (2%)
    pallas_call x1, Pallas kernels, on_device(): pl.pallas_call(whole_kernel, in_specs=[VM, VM, ANY, ANY, VM, ANY, ANY], o...  71.7 us
    pallas_call x1, Pallas kernels, on_device(): pl.pallas_call(last_kernel, in_specs=[ANY, ANY, VM] + [ANY] * 4, out_spec...  38.2 us
    unnamed x2, local copies, waits for them, and re-layouts  2.7 us

profile of v3, /device:TPU:4, one launch (start us, length us, event | category | flops | bytes accessed | tf_op | source)
XLA Modules:
  0.0 113.3 jit_solution(6281630744678229106)
XLA Ops:
  0.6 1.3 %copy.12.nb_any = s32[8,4]{1,0:T(8,128)} copy(s32[8,4]{0,1:T(4,128)} %param.12) | data formatting | bytes 256 | tf_op args[5]
  2.0 1.3 %copy.13.ed_any = s32[8,4]{1,0:T(8,128)} copy(s32[8,4]{0,1:T(4,128)} %param.13) | data formatting | bytes 256 | tf_op args[6]
  3.3 71.7 %shard_map.110 = (bf16[8,256,256]{2,1,0:T(8,128)(2,1)}, f32[8,256,256]{2,1,0:T(8,128)}, f32[9,8,256]{2,1,0:T(8,128)}, f32[9,8,256]{2,1,0:T(8,128)}, f32[1,256]{1,0:T(1,128)}, /*index=5*/f32[8,256]{1,0:T(8,128)}) custom-call(bf16[8,256,256]{2,1,0:T(8,128)(2,1)} %bitcast.6, bf16[8,256,256]{2,1,0:T(8,128)(2,1)} %bitcast.8, bf16[9,256,256]{2,1,0:T(8,128)(2,1)} %wf_any.1, ...), custom_call_target="tpu_custom_call" | custom-call | tf_op jit(solution)/shard_map/pallas_call | solution.py:926
  75.0 38.2 %shard_map.111 = (bf16[8,256,256]{2,1,0:T(8,128)(2,1)}, f32[8,256,256]{2,1,0:T(8,128)}, f32[9,8,256]{2,1,0:T(8,128)}, f32[9,8,256]{2,1,0:T(8,128)}, f32[1,256]{1,0:T(1,128)}) custom-call(bf16[8,256,256]{2,1,0:T(8,128)(2,1)} %bitcast.7, f32[8,256,256]{2,1,0:T(8,128)} %get-tuple-element.16.ga, f32[8,256]{1,0:T(8,128)} %get-tuple-element.17.vectors, ...), custom_call_target="tpu_custom_call" | custom-call | tf_op jit(solution)/shard_map/pallas_call | solution.py:939

commit v4 on v3

--- a/solution.py
+++ b/solution.py
@@ -251,7 +251,7 @@
             @pl.loop(0, SLOTS)
             def _(slot):
                 face, edge = lax.div(slot, 2), 2 * lax.rem(slot, 2)
-                source = 2 * self.nb[face, edge] + lax.div(self.ed[face, edge], 2)
+                source = 2 * self.nb[edge, face] + lax.div(self.ed[edge, face], 2)
                 self.st[slot] = self.r1[source]
 
             @pl.loop(1, SLOTS)
@@ -303,7 +303,7 @@
         copies = remote(arrived, arrived, self.ss, self.sr, other, self.tile)
         copies.wait_recv()
         copies.wait_send()
-        left_face, right_face = self.nb[self.face, 3], self.nb[self.face, 1]
+        left_face, right_face = self.nb[3, self.face], self.nb[1, self.face]
         self.sides[0:16, :] = self.sall[left_face, 16:32, :]
         self.sides[16:32, :] = self.sall[right_face, 0:16, :]
 
@@ -370,8 +370,8 @@
 def edge_flags(ed_ref):
     face, tile = place()
     first, last = tile == 0, tile == NT - 1
-    flip_top = first & (ed_ref[face, 0] != 2)
-    flip_bottom = last & (ed_ref[face, 2] != 0)
+    flip_top = first & (ed_ref[0, face] != 2)
+    flip_bottom = last & (ed_ref[2, face] != 0)
     return first, last, flip_top, flip_bottom
 
 
@@ -646,8 +646,8 @@
 ANY = pl.BlockSpec(memory_space=pl.ANY)
 
 WORK_SCRATCH = [
-    pltpu.SMEM((NF, 4), jnp.int32),
-    pltpu.SMEM((NF, 4), jnp.int32),
+    pltpu.SMEM((4, NF), jnp.int32),
+    pltpu.SMEM((4, NF), jnp.int32),
     pltpu.VMEM((9, C, C), BF),
     pltpu.VMEM((9, C, C), BF),
     pltpu.VMEM((HALF, CS, C), BF),
@@ -869,35 +869,29 @@
 
 
 def last_kernel(
-    feat, ga, vectors, output_in, wf_in, wc_in, gain_in,
-    output, grad_features, wf_out, wc_out, gain_out, feat_v, ga_v, out_v, sems
+    feat, ga, vectors, wf_in, wc_in, gain_in, output_in,
+    output, grad_features, wf_out, wc_out, gain_out, feat_v, ga_v, sum_v, out_v, sems
 ):
-    passed = [
-        pltpu.make_async_copy(src, dst, sems.at[i])
-        for i, (src, dst) in enumerate(
-            ((output_in, output), (wf_in, wf_out), (wc_in, wc_out), (gain_in, gain_out))
-        )
-    ]
-
-    def rows(q):
-        return pl.ds(2 * q, 2)
-
-    loads = [
-        (
-            pltpu.make_async_copy(feat.at[rows(q)], feat_v.at[rows(q)], sems.at[4 + 3 * q]),
-            pltpu.make_async_copy(ga.at[rows(q)], ga_v.at[rows(q)], sems.at[5 + 3 * q]),
-        )
-        for q in range(HALF)
-    ]
-    stores = [
-        pltpu.make_async_copy(out_v.at[rows(q)], grad_features.at[rows(q)], sems.at[6 + 3 * q])
-        for q in range(HALF)
-    ]
-    for load in loads:
-        for copy in load:
+    def rows(ref, q):
+        return ref.at[pl.ds(2 * q, 2)]
+
+    def moves(pairs, first):
+        return [
+            [
+                pltpu.make_async_copy(rows(src, q), rows(dst, q), sems.at[first + i, q])
+                for i, (src, dst) in enumerate(pairs)
+            ]
+            for q in range(HALF)
+        ]
+
+    loads = moves(((feat, feat_v), (ga, ga_v), (output_in, sum_v)), 0)
+    stores = moves(((out_v, grad_features), (sum_v, output)), 3)
+    for chunk in loads:
+        for copy in chunk:
             copy.start()
-    for copy in passed:
-        copy.start()
+    wf_out[...] = wf_in[...]
+    wc_out[...] = wc_in[...]
+    gain_out[...] = gain_in[...]
     mean, inverse, scale = vectors[0:1], vectors[1:2], vectors[2:3]
     group_shift, group_slope = vectors[3:4], vectors[4:5]
     for q in range(HALF):
@@ -906,9 +900,11 @@
         for r in (2 * q, 2 * q + 1):
             normed = (feat_v[r].astype(F32) - mean) * inverse
             out_v[r] = inverse * (scale * ga_v[r] - group_shift - normed * group_slope)
-        stores[q].start()
-    for copy in stores + passed:
-        copy.wait()
+        for copy in stores[q]:
+            copy.start()
+    for chunk in stores:
+        for copy in chunk:
+            copy.wait()
 
 
 def shape(dims, dtype):
@@ -935,20 +931,21 @@
         compiler_params=pltpu.CompilerParams(
             vmem_limit_bytes=VMEM_LIMIT, collective_id=1, has_side_effects=True
         ),
-    )(features[0], cotangent[0], w_fine, w_coarse, gain[None], neighbors, neighbor_edges)
+    )(features[0], cotangent[0], w_fine, w_coarse, gain[None], neighbors.T, neighbor_edges.T)
     output, grad_features, grad_w_fine, grad_w_coarse, grad_gain = pl.pallas_call(
         last_kernel,
-        in_specs=[ANY, ANY, VM] + [ANY] * 4,
-        out_specs=[ANY] * 5,
+        in_specs=[ANY, ANY] + [VM] * 4 + [ANY],
+        out_specs=[ANY, ANY] + [VM] * 3,
         out_shape=outs,
         scratch_shapes=[
             pltpu.VMEM((RD, FS, C), BF),
             pltpu.VMEM((RD, FS, C), F32),
+            pltpu.VMEM((RD, FS, C), BF),
             pltpu.VMEM((RD, FS, C), F32),
-            DMA((4 + 3 * HALF,)),
+            DMA((5, HALF)),
         ],
         compiler_params=pltpu.CompilerParams(vmem_limit_bytes=VMEM_LIMIT),
-    )(features[0], grad_act, vectors, output, grad_w_fine, grad_w_coarse, grad_gain)
+    )(features[0], grad_act, vectors, grad_w_fine, grad_w_coarse, grad_gain, output)
     return (output[None], grad_features[None], grad_w_fine, grad_w_coarse, grad_gain[0])
 
 

time: 113 us -> 77.6 us (0.69)
  Pallas kernels: 110 us -> 76.8 us
  local copies, waits for them, and re-layouts: 2.7 us -> 0 us
    pallas_call x1, Pallas kernels: 38.2 us -> 4.92 us  [on_device(): pl.pallas_call(last_kernel, in_specs=[ANY, ANY] + [VM] * 4 + [ANY], out_s...]
    unnamed x2 -> x0, local copies, waits for them, and re-layouts: 2.7 us -> none
where the time goes in v4:
time: 77.6 us; the launch traced here: 77.4 us
  Pallas kernels  76.8 us (99%)
    pallas_call x1, Pallas kernels, on_device(): pl.pallas_call(whole_kernel, in_specs=[VM, VM, ANY, ANY, VM, ANY, ANY], o...  71.8 us
    pallas_call x1, Pallas kernels, on_device(): pl.pallas_call(last_kernel, in_specs=[ANY, ANY] + [VM] * 4 + [ANY], out_s...  4.92 us

profile of v4, /device:TPU:4, one launch (start us, length us, event | category | flops | bytes accessed | tf_op | source)
XLA Modules:
  0.0 77.4 jit_solution(5322102501435943735)
XLA Ops:
  0.6 71.8 %shard_map.110 = (bf16[8,256,256]{2,1,0:T(8,128)(2,1)}, f32[8,256,256]{2,1,0:T(8,128)}, f32[9,8,256]{2,1,0:T(8,128)}, f32[9,8,256]{2,1,0:T(8,128)}, f32[1,256]{1,0:T(1,128)}, /*index=5*/f32[8,256]{1,0:T(8,128)}) custom-call(bf16[8,256,256]{2,1,0:T(8,128)(2,1)} %bitcast.8, bf16[8,256,256]{2,1,0:T(8,128)(2,1)} %bitcast.10, bf16[9,256,256]{2,1,0:T(8,128)(2,1)} %wf_any.1, ...), custom_call_target="tpu_custom_call" | custom-call | tf_op jit(solution)/shard_map/pallas_call | solution.py:922
  72.5 4.9 %shard_map.111 = (bf16[8,256,256]{2,1,0:T(8,128)(2,1)}, f32[8,256,256]{2,1,0:T(8,128)}, f32[9,8,256]{2,1,0:T(8,128)}, f32[9,8,256]{2,1,0:T(8,128)}, f32[1,256]{1,0:T(1,128)}) custom-call(bf16[8,256,256]{2,1,0:T(8,128)(2,1)} %bitcast.9, f32[8,256,256]{2,1,0:T(8,128)} %get-tuple-element.16.ga, f32[8,256]{1,0:T(8,128)} %get-tuple-element.17.vectors, ...), custom_call_target="tpu_custom_call" | custom-call | tf_op jit(solution)/shard_map/pallas_call | solution.py:935

commit v5 on v4

--- a/solution.py
+++ b/solution.py
@@ -415,8 +415,8 @@
 
 
 def put_share(shares, tap, product):
-    turned = product.T.reshape(4, 4, 2, 8, C)
-    halves = [turned[..., :128], turned[..., 128:]]
+    cut = product.reshape(4, 4, 2, 8, C)
+    halves = [cut[..., :128], cut[..., 128:]]
     shares[:, :, :, 16 * tap : 16 * tap + 16, :] = jnp.concatenate(halves, axis=3).astype(BF)
 
 
@@ -701,7 +701,7 @@
     halo1_scratch, halo2_scratch = take(N_HALO), take(N_HALO)
     (
         nb, ed, wf_taps, wc_taps, gco, wtf, wtc, x3, u3, c3, v3, fine, coarse_in, grad_fine,
-        ga, gci, gt, gct, edge_h, edge_c, local,
+        ga, gci, gt, ct, edge_h, edge_c, local,
     ) = take(len(WORK_SCRATCH))
     reduce_f = Reduce(take(len(REDUCE_SCRATCH)))
     reduce_c = Reduce(take(len(REDUCE_SCRATCH)))
@@ -739,8 +739,6 @@
     sum_start(line_b, own_b, buf_b, sb, rb)
     halo1.middle()
     back_weights(wf_taps, wtf)
-    for r in range(HALF):
-        gct[:, r * CS : (r + 1) * CS] = gco[r].astype(F32).T.astype(BF)
 
     first, last, flip_top, flip_bottom = edge_flags(ed)
     halo1.finish((flip_top, flip_bottom))
@@ -786,32 +784,53 @@
     halo2.start()
     pl.loop(1, HALF - 1)(forward)
 
+    for r in range(HALF):
+        ct[:, r * CS : (r + 1) * CS] = coarse_in[r].astype(F32).T.astype(BF)
+    inner = (HALF - 1) * CS
+    over_top = dot(ct[:, 0:CS], v3[0])
+    over_bottom = dot(ct[:, inner:], v3[HALF + 1])
+
+    def block(product, m):
+        return product[:, m * C : (m + 1) * C]
+
+    for k in (2, 1, 0):
+        if k == 0:
+            product = dot(ct[:, CS:], rows_of(v3, 1, HALF - 1))
+        elif k == 1:
+            product = dot(ct[...], rows_of(v3, 1, HALF))
+        else:
+            product = dot(ct[:, 0:inner], rows_of(v3, 2, HALF - 1))
+        for m in range(3):
+            term = block(product, m)
+            if k == 0:
+                term += jnp.where(flip_top, 0.0, block(over_top, m))
+                term += jnp.where(flip_bottom, block(over_bottom, 2 - m), 0.0)
+            elif k == 2:
+                term += jnp.where(flip_bottom, 0.0, block(over_bottom, m))
+                term += jnp.where(flip_top, block(over_top, 2 - m), 0.0)
+            put_share(reduce_c.shares, 8 - (3 * k + m), term)
+        reduce_c.swap_start(2 - k)
+
     def fine_gradient(k):
         product = dot(gt[...], rows_of(x3, k, RD))
         for m in range(3):
-            put_share(reduce_f.shares, 3 * k + m, product[:, m * C : (m + 1) * C])
+            put_share(reduce_f.shares, 3 * k + m, block(product, m).T)
         reduce_f.swap_start(k)
 
     for r in range(RD):
         gt[:, r * FS : (r + 1) * FS] = grad_fine[r].astype(F32).T.astype(BF)
+    fine_gradient(0)
     halo2.middle()
-    for k in range(3):
-        fine_gradient(k)
+    fine_gradient(1)
+    reduce_c.swap_take()
+    fine_gradient(2)
     halo2.finish((flip_top, flip_bottom))
     edge_h[...] = masked_sides(halo2.sides[...].astype(F32), first, last)
     reduce_f.swap_take()
 
-    extended(c3, coarse_in, halo2.hc, edge_h, RD + 2, lambda row: row)
-    for k in range(3):
-        product = dot(gct[...], rows_of(c3, k, HALF))
-        for m in range(3):
-            put_share(reduce_c.shares, 3 * k + m, product[:, m * C : (m + 1) * C])
-        reduce_c.swap_start(k)
-    reduce_f.first_take()
-
     extended(u3, grad_fine, halo2.hf, edge_h, 0, lambda row: row)
     top, bottom = halo_weights(wtf, flip_top, flip_bottom)
-    reduce_c.swap_take()
+    reduce_c.first_take()
     ga[1 : RD - 1] = jnp.zeros((RD - 2, FS, C), F32)
     ga[0] = dot(u3[0], top)
     ga[RD - 1] = dot(u3[RD + 1], bottom)
@@ -832,13 +851,18 @@
         own_c[1:2, :] += jnp.sum(grad, axis=0, keepdims=True)
 
     pl.loop(0, HALF // 2)(back)
-    reduce_f.second_take()
-    reduce_c.first_take()
+    reduce_f.first_take()
+    reduce_c.second_take()
     pl.loop(HALF // 2, HALF)(back)
     sum_start(line_a, own_c, buf_c, sc, rc)
     store_act = pltpu.make_async_copy(ga, grad_act, local.at[4])
     store_act.start()
-    reduce_c.second_take()
+    reduce_f.second_take()
+
+    extended(c3, coarse_in, halo2.hc, edge_h, RD + 2, lambda row: row)
+    own_d[...] = sum_finish(line_a, own_c, buf_c, sc, rc)
+    sum_start(line_b, own_d, buf_d, sd, rd)
+    reduce_c.chips_take()
 
     @pl.loop(0, HALF)
     def _(i):
@@ -851,10 +875,7 @@
 
     store_output = pltpu.make_async_copy(fine, output, local.at[5])
     store_output.start()
-    own_d[...] = sum_finish(line_a, own_c, buf_c, sc, rc)
-    sum_start(line_b, own_d, buf_d, sd, rd)
     reduce_f.chips_take()
-    reduce_c.chips_take()
     sums = sum_finish(line_b, own_d, buf_d, sd, rd)
 
     grad_gain[...] = sums[0:1] * (1.0 / CELLS)
@@ -862,8 +883,8 @@
     group_slope, group_shift = grouped[0:1], grouped[1:2]
     for i, vector in enumerate((mean, inverse, scale, group_shift, group_slope)):
         vectors[i : i + 1, :] = vector
+    reduce_c.finish(grad_w_coarse)
     reduce_f.finish(grad_w_fine)
-    reduce_c.finish(grad_w_coarse)
     store_act.wait()
     store_output.wait()
 

time: 77.6 us -> 74.5 us (0.960)
  Pallas kernels: 76.8 us -> 73.4 us
    pallas_call x1, Pallas kernels: 71.8 us -> 68.5 us  [on_device(): pl.pallas_call(whole_kernel, in_specs=[VM, VM, ANY, ANY, VM, ANY, ANY], o...]
where the time goes in v5:
time: 74.5 us; the launch traced here: 74 us
  Pallas kernels  73.4 us (99%)
    pallas_call x1, Pallas kernels, on_device(): pl.pallas_call(whole_kernel, in_specs=[VM, VM, ANY, ANY, VM, ANY, ANY], o...  68.5 us
    pallas_call x1, Pallas kernels, on_device(): pl.pallas_call(last_kernel, in_specs=[ANY, ANY] + [VM] * 4 + [ANY], out_s...  4.92 us

profile of v5, /device:TPU:4, one launch (start us, length us, event | category | flops | bytes accessed | tf_op | source)
XLA Modules:
  0.0 74.0 jit_solution(13706560176442973880)
XLA Ops:
  0.6 68.5 %shard_map.110 = (bf16[8,256,256]{2,1,0:T(8,128)(2,1)}, f32[8,256,256]{2,1,0:T(8,128)}, f32[9,8,256]{2,1,0:T(8,128)}, f32[9,8,256]{2,1,0:T(8,128)}, f32[1,256]{1,0:T(1,128)}, /*index=5*/f32[8,256]{1,0:T(8,128)}) custom-call(bf16[8,256,256]{2,1,0:T(8,128)(2,1)} %bitcast.8, bf16[8,256,256]{2,1,0:T(8,128)(2,1)} %bitcast.10, bf16[9,256,256]{2,1,0:T(8,128)(2,1)} %wf_any.1, ...), custom_call_target="tpu_custom_call" | custom-call | tf_op jit(solution)/shard_map/pallas_call | solution.py:943
  69.1 4.9 %shard_map.111 = (bf16[8,256,256]{2,1,0:T(8,128)(2,1)}, f32[8,256,256]{2,1,0:T(8,128)}, f32[9,8,256]{2,1,0:T(8,128)}, f32[9,8,256]{2,1,0:T(8,128)}, f32[1,256]{1,0:T(1,128)}) custom-call(bf16[8,256,256]{2,1,0:T(8,128)(2,1)} %bitcast.9, f32[8,256,256]{2,1,0:T(8,128)} %get-tuple-element.16.ga, f32[8,256]{1,0:T(8,128)} %get-tuple-element.17.vectors, ...), custom_call_target="tpu_custom_call" | custom-call | tf_op jit(solution)/shard_map/pallas_call | solution.py:956

commit v6 on v5

--- a/solution.py
+++ b/solution.py
@@ -687,7 +687,7 @@
 
 def whole_kernel(
     feat, cot, wf_any, wc_any, gain, nb_any, ed_any,
-    output, grad_act, grad_w_fine, grad_w_coarse, grad_gain, vectors, *scratch
+    output, grad_features, grad_w_fine, grad_w_coarse, grad_gain, *scratch
 ):
     scratch = list(scratch)
 
@@ -855,8 +855,6 @@
     reduce_c.second_take()
     pl.loop(HALF // 2, HALF)(back)
     sum_start(line_a, own_c, buf_c, sc, rc)
-    store_act = pltpu.make_async_copy(ga, grad_act, local.at[4])
-    store_act.start()
     reduce_f.second_take()
 
     extended(c3, coarse_in, halo2.hc, edge_h, RD + 2, lambda row: row)
@@ -875,23 +873,30 @@
 
     store_output = pltpu.make_async_copy(fine, output, local.at[5])
     store_output.start()
-    reduce_f.chips_take()
     sums = sum_finish(line_b, own_d, buf_d, sd, rd)
 
     grad_gain[...] = sums[0:1] * (1.0 / CELLS)
     grouped = group_sum(sums * scale) / (CELLS * GROUP)
     group_slope, group_shift = grouped[0:1], grouped[1:2]
-    for i, vector in enumerate((mean, inverse, scale, group_shift, group_slope)):
-        vectors[i : i + 1, :] = vector
+
+    @pl.loop(0, RD)
+    def _(r):
+        normed = (feat[r].astype(F32) - mean) * inverse
+        grad = inverse * (scale * ga[r] - group_shift - normed * group_slope)
+        grad_fine[r] = grad.astype(BF)
+
+    store_features = pltpu.make_async_copy(grad_fine, grad_features, local.at[4])
+    store_features.start()
+    reduce_f.chips_take()
     reduce_c.finish(grad_w_coarse)
     reduce_f.finish(grad_w_fine)
-    store_act.wait()
+    store_features.wait()
     store_output.wait()
 
 
 def last_kernel(
-    feat, ga, vectors, wf_in, wc_in, gain_in, output_in,
-    output, grad_features, wf_out, wc_out, gain_out, feat_v, ga_v, sum_v, out_v, sems
+    features_in, output_in, wf_in, wc_in, gain_in,
+    output, grad_features, wf_out, wc_out, gain_out, narrow, sum_v, wide, sems
 ):
     def rows(ref, q):
         return ref.at[pl.ds(2 * q, 2)]
@@ -905,24 +910,20 @@
             for q in range(HALF)
         ]
 
-    loads = moves(((feat, feat_v), (ga, ga_v), (output_in, sum_v)), 0)
-    stores = moves(((out_v, grad_features), (sum_v, output)), 3)
+    loads = moves(((features_in, narrow), (output_in, sum_v)), 0)
+    stores = moves(((wide, grad_features), (sum_v, output)), 2)
     for chunk in loads:
         for copy in chunk:
             copy.start()
     wf_out[...] = wf_in[...]
     wc_out[...] = wc_in[...]
     gain_out[...] = gain_in[...]
-    mean, inverse, scale = vectors[0:1], vectors[1:2], vectors[2:3]
-    group_shift, group_slope = vectors[3:4], vectors[4:5]
     for q in range(HALF):
-        for copy in loads[q]:
-            copy.wait()
-        for r in (2 * q, 2 * q + 1):
-            normed = (feat_v[r].astype(F32) - mean) * inverse
-            out_v[r] = inverse * (scale * ga_v[r] - group_shift - normed * group_slope)
-        for copy in stores[q]:
-            copy.start()
+        for load, store in zip(loads[q], stores[q]):
+            load.wait()
+            if store is stores[q][0]:
+                wide[2 * q : 2 * q + 2] = narrow[2 * q : 2 * q + 2].astype(F32)
+            store.start()
     for chunk in stores:
         for copy in chunk:
             copy.wait()
@@ -940,11 +941,12 @@
         shape((9, 8, C), F32),
         shape((1, C), F32),
     ]
-    output, grad_act, grad_w_fine, grad_w_coarse, grad_gain, vectors = pl.pallas_call(
+    narrow = [outs[0], shape((RD, FS, C), BF)] + outs[2:]
+    output, grad_features, grad_w_fine, grad_w_coarse, grad_gain = pl.pallas_call(
         whole_kernel,
         in_specs=[VM, VM, ANY, ANY, VM, ANY, ANY],
-        out_specs=[ANY, ANY, VM, VM, VM, VM],
-        out_shape=outs + [shape((8, C), F32)],
+        out_specs=[ANY, ANY, VM, VM, VM],
+        out_shape=narrow,
         scratch_shapes=SUM_SCRATCH * 2
         + HALO_SCRATCH * 2
         + WORK_SCRATCH
@@ -955,18 +957,17 @@
     )(features[0], cotangent[0], w_fine, w_coarse, gain[None], neighbors.T, neighbor_edges.T)
     output, grad_features, grad_w_fine, grad_w_coarse, grad_gain = pl.pallas_call(
         last_kernel,
-        in_specs=[ANY, ANY] + [VM] * 4 + [ANY],
+        in_specs=[ANY, ANY] + [VM] * 3,
         out_specs=[ANY, ANY] + [VM] * 3,
         out_shape=outs,
         scratch_shapes=[
             pltpu.VMEM((RD, FS, C), BF),
-            pltpu.VMEM((RD, FS, C), F32),
             pltpu.VMEM((RD, FS, C), BF),
             pltpu.VMEM((RD, FS, C), F32),
-            DMA((5, HALF)),
+            DMA((4, HALF)),
         ],
         compiler_params=pltpu.CompilerParams(vmem_limit_bytes=VMEM_LIMIT),
-    )(features[0], grad_act, vectors, grad_w_fine, grad_w_coarse, grad_gain, output)
+    )(grad_features, output, grad_w_fine, grad_w_coarse, grad_gain)
     return (output[None], grad_features[None], grad_w_fine, grad_w_coarse, grad_gain[0])
 
 

time: 74.5 us -> 77.2 us (1.036)
  Pallas kernels: 73.4 us -> 76.3 us
    pallas_call x1, Pallas kernels: 68.5 us -> 72 us  [on_device(): pl.pallas_call(whole_kernel, in_specs=[VM, VM, ANY, ANY, VM, ANY, ANY], o...]
where the time goes in v6:
time: 77.2 us; the launch traced here: 77 us
  Pallas kernels  76.3 us (99%)
    pallas_call x1, Pallas kernels, on_device(): pl.pallas_call(whole_kernel, in_specs=[VM, VM, ANY, ANY, VM, ANY, ANY], o...  72 us
    pallas_call x1, Pallas kernels, on_device(): pl.pallas_call(last_kernel, in_specs=[ANY, ANY] + [VM] * 3, out_specs=[AN...  4.36 us

profile of v6, /device:TPU:4, one launch (start us, length us, event | category | flops | bytes accessed | tf_op | source)
XLA Modules:
  0.0 77.0 jit_solution(3624147614840517340)
XLA Ops:
  0.6 72.0 %shard_map.110 = (bf16[8,256,256]{2,1,0:T(8,128)(2,1)}, bf16[8,256,256]{2,1,0:T(8,128)(2,1)}, f32[9,8,256]{2,1,0:T(8,128)}, f32[9,8,256]{2,1,0:T(8,128)}, f32[1,256]{1,0:T(1,128)}) custom-call(bf16[8,256,256]{2,1,0:T(8,128)(2,1)} %bitcast.8, bf16[8,256,256]{2,1,0:T(8,128)(2,1)} %bitcast.9, bf16[9,256,256]{2,1,0:T(8,128)(2,1)} %wf_any.1, ...), custom_call_target="tpu_custom_call" | custom-call | tf_op jit(solution)/shard_map/pallas_call | solution.py:945
  72.6 4.4 %shard_map.111 = (bf16[8,256,256]{2,1,0:T(8,128)(2,1)}, f32[8,256,256]{2,1,0:T(8,128)}, f32[9,8,256]{2,1,0:T(8,128)}, f32[9,8,256]{2,1,0:T(8,128)}, f32[1,256]{1,0:T(1,128)}) custom-call(bf16[8,256,256]{2,1,0:T(8,128)(2,1)} %get-tuple-element.15.features_in, bf16[8,256,256]{2,1,0:T(8,128)(2,1)} %get-tuple-element.16.output_in, ...), custom_call_target="tpu_custom_call" | custom-call | tf_op jit(solution)/shard_map/pallas_call | solution.py:958

commit v7 on v6

--- a/solution.py
+++ b/solution.py
@@ -648,6 +648,8 @@
 WORK_SCRATCH = [
     pltpu.SMEM((4, NF), jnp.int32),
     pltpu.SMEM((4, NF), jnp.int32),
+    pltpu.VMEM((RD, FS, C), BF),
+    pltpu.VMEM((RD, FS, C), BF),
     pltpu.VMEM((9, C, C), BF),
     pltpu.VMEM((9, C, C), BF),
     pltpu.VMEM((HALF, CS, C), BF),
@@ -666,7 +668,7 @@
     pltpu.VMEM((C, HALF * CS), BF),
     pltpu.VMEM((32, C), F32),
     pltpu.VMEM((32, C), F32),
-    DMA((6,)),
+    DMA((8,)),
 ]
 
 
@@ -686,7 +688,7 @@
 
 
 def whole_kernel(
-    feat, cot, wf_any, wc_any, gain, nb_any, ed_any,
+    feat_any, cot_any, wf_any, wc_any, gain, nb_any, ed_any,
     output, grad_features, grad_w_fine, grad_w_coarse, grad_gain, *scratch
 ):
     scratch = list(scratch)
@@ -700,25 +702,34 @@
     own_c, own_d, buf_c, buf_d, sc, rc, sd, rd = take(N_SUM)
     halo1_scratch, halo2_scratch = take(N_HALO), take(N_HALO)
     (
-        nb, ed, wf_taps, wc_taps, gco, wtf, wtc, x3, u3, c3, v3, fine, coarse_in, grad_fine,
+        nb, ed, feat, cot, wf_taps, wc_taps, gco, wtf, wtc, x3, u3, c3, v3, fine, coarse_in, grad_fine,
         ga, gci, gt, ct, edge_h, edge_c, local,
     ) = take(len(WORK_SCRATCH))
     reduce_f = Reduce(take(len(REDUCE_SCRATCH)))
     reduce_c = Reduce(take(len(REDUCE_SCRATCH)))
 
-    barrier_signal()
     loads = [
         pltpu.make_async_copy(src, dst, local.at[i])
         for i, (src, dst) in enumerate(
-            ((nb_any, nb), (ed_any, ed), (wf_any, wf_taps), (wc_any, wc_taps))
+            (
+                (feat_any, feat),
+                (cot_any, cot),
+                (nb_any, nb),
+                (ed_any, ed),
+                (wc_any, wc_taps),
+                (wf_any, wf_taps),
+            )
         )
     ]
     for load in loads:
         load.start()
+    barrier_signal()
     halo1 = Halo(feat, gco, halo1_scratch, (nb, ed))
     halo2 = Halo(grad_fine, coarse_in, halo2_scratch, (nb, ed))
 
     pool, widen = pool_matrix(), spread_matrix()
+    for load in loads[:2]:
+        load.wait()
     own_a[...] = jnp.zeros_like(own_a)
     own_c[...] = jnp.zeros_like(own_c)
 
@@ -732,7 +743,7 @@
     barrier_wait()
     sum_start(line_a, own_a, buf_a, sa, ra)
     halo1.start()
-    for load in loads:
+    for load in loads[2:]:
         load.wait()
     back_weights(wc_taps, wtc)
     own_b[...] = sum_finish(line_a, own_a, buf_a, sa, ra)
@@ -871,8 +882,9 @@
         for r in range(2):
             fine[2 * i + r] = (fine[2 * i + r].astype(F32) + wide).astype(BF)
 
-    store_output = pltpu.make_async_copy(fine, output, local.at[5])
+    store_output = pltpu.make_async_copy(fine, output, local.at[7])
     store_output.start()
+    reduce_f.chips_take()
     sums = sum_finish(line_b, own_d, buf_d, sd, rd)
 
     grad_gain[...] = sums[0:1] * (1.0 / CELLS)
@@ -885,9 +897,8 @@
         grad = inverse * (scale * ga[r] - group_shift - normed * group_slope)
         grad_fine[r] = grad.astype(BF)
 
-    store_features = pltpu.make_async_copy(grad_fine, grad_features, local.at[4])
+    store_features = pltpu.make_async_copy(grad_fine, grad_features, local.at[6])
     store_features.start()
-    reduce_f.chips_take()
     reduce_c.finish(grad_w_coarse)
     reduce_f.finish(grad_w_fine)
     store_features.wait()
@@ -944,7 +955,7 @@
     narrow = [outs[0], shape((RD, FS, C), BF)] + outs[2:]
     output, grad_features, grad_w_fine, grad_w_coarse, grad_gain = pl.pallas_call(
         whole_kernel,
-        in_specs=[VM, VM, ANY, ANY, VM, ANY, ANY],
+        in_specs=[ANY] * 4 + [VM] + [ANY] * 2,
         out_specs=[ANY, ANY, VM, VM, VM],
         out_shape=narrow,
         scratch_shapes=SUM_SCRATCH * 2

time: 77.2 us -> 73 us (0.946)
  Pallas kernels: 76.3 us -> 71.9 us
    pallas_call x1, Pallas kernels: 72 us -> 67.5 us  [on_device(): pl.pallas_call(whole_kernel, in_specs=[ANY] * 4 + [VM] + [ANY] * 2, out_s...]
where the time goes in v7:
time: 73 us; the launch traced here: 72.5 us
  Pallas kernels  71.9 us (98%)
    pallas_call x1, Pallas kernels, on_device(): pl.pallas_call(whole_kernel, in_specs=[ANY] * 4 + [VM] + [ANY] * 2, out_s...  67.5 us
    pallas_call x1, Pallas kernels, on_device(): pl.pallas_call(last_kernel, in_specs=[ANY, ANY] + [VM] * 3, out_specs=[AN...  4.36 us

profile of v7, /device:TPU:4, one launch (start us, length us, event | category | flops | bytes accessed | tf_op | source)
XLA Modules:
  0.0 72.5 jit_solution(4335779526250217767)
XLA Ops:
  0.6 67.5 %shard_map.110 = (bf16[8,256,256]{2,1,0:T(8,128)(2,1)}, bf16[8,256,256]{2,1,0:T(8,128)(2,1)}, f32[9,8,256]{2,1,0:T(8,128)}, f32[9,8,256]{2,1,0:T(8,128)}, f32[1,256]{1,0:T(1,128)}) custom-call(bf16[8,256,256]{2,1,0:T(8,128)(2,1)} %bitcast.8, bf16[8,256,256]{2,1,0:T(8,128)(2,1)} %bitcast.9, bf16[9,256,256]{2,1,0:T(8,128)(2,1)} %wf_any.1, ...), custom_call_target="tpu_custom_call" | custom-call | tf_op jit(solution)/shard_map/pallas_call | solution.py:956
  68.2 4.4 %shard_map.111 = (bf16[8,256,256]{2,1,0:T(8,128)(2,1)}, f32[8,256,256]{2,1,0:T(8,128)}, f32[9,8,256]{2,1,0:T(8,128)}, f32[9,8,256]{2,1,0:T(8,128)}, f32[1,256]{1,0:T(1,128)}) custom-call(bf16[8,256,256]{2,1,0:T(8,128)(2,1)} %get-tuple-element.15.features_in, bf16[8,256,256]{2,1,0:T(8,128)(2,1)} %get-tuple-element.16.output_in, ...), custom_call_target="tpu_custom_call" | custom-call | tf_op jit(solution)/shard_map/pallas_call | solution.py:969
